TPU v7x, 512 devices: a whole 4x4x16 slice. The times are simulated.
512 devices in a mesh: ep: 64 (over x_hi, z, core), edp: 8 (over x_lo, y).
Axes of the slice: x: 4 (x_hi: 2, x_lo: 2; x = x_hi * 2 + x_lo), y: 4, z: 16, core: 2. Of those that a mesh axis runs over, the one named last changes fastest.
Arguments:
- dense_acts: bfloat16 [327680, 512], P(('ep', 'edp')), may hold values from -6 to 6
- dense_cot: bfloat16 [327680, 1536], P(('ep', 'edp')), may hold values from -6 to 6
- advantage: float32 [327680], P(('ep', 'edp')), may hold values from -5 to 5
- dense_master: float32 [512, 1536], P(('ep', 'edp')), may hold values from -0.6 to 0.6
- dense_first: float32 [512, 1536], P(('ep', 'edp')), may hold values from -0.1 to 0.1
- dense_second: float32 [512, 1536], P(('ep', 'edp')), may hold values from 0.002 to 0.1
- routed_grads: bfloat16 [8, 256, 8, 2048], P('edp', 'ep'), may hold values from -6 to 6
- routed_master: float32 [256, 8, 2048], P('ep', 'edp'), may hold values from -0.6 to 0.6
- routed_first: float32 [256, 8, 2048], P('ep', 'edp'), may hold values from -0.1 to 0.1
- routed_second: float32 [256, 8, 2048], P('ep', 'edp'), may hold values from 0.002 to 0.1
Outputs:
- dense_master_new: float32 [512, 1536], P(('ep', 'edp'))
- dense_first_new: float32 [512, 1536], P(('ep', 'edp'))
- dense_second_new: float32 [512, 1536], P(('ep', 'edp'))
- dense_weights: bfloat16 [512, 1536], replicated
- routed_master_new: float32 [256, 8, 2048], P('ep', 'edp')
- routed_first_new: float32 [256, 8, 2048], P('ep', 'edp')
- routed_second_new: float32 [256, 8, 2048], P('ep', 'edp')
- routed_weights: bfloat16 [256, 8, 2048], P('ep')
All inputs are finite; a program needn't handle non-finite values.
Results may differ from a plain program's by a relative error of at most 0.0034.
Values may be sent and summed in bfloat16 or wider, within the bound.
No kernel may reach another device: no remote copies, remote signals or barrier semaphores. Data moves between devices by JAX's collectives and lax.ppermute only.
A program may use at most 64 MiB of HBM per device.

v0:
```python
import math

import jax
import jax.numpy as jnp
from jax import lax
from jax.sharding import PartitionSpec as P

beta_one = 0.9
beta_two = 0.95
learn_rate = 0.001
decay_rate = 0.1
epsilon = 1e-08


def adamw_update(gradient, master, first_moment, second_moment):
    first_new = beta_one * first_moment + (1.0 - beta_one) * gradient
    second_new = beta_two * second_moment + (1.0 - beta_two) * gradient * gradient
    master_new = master - learn_rate * (
        first_new / (jnp.sqrt(second_new) + epsilon) + decay_rate * master
    )
    return (master_new, first_new, second_new)


def per_device(
    dense_acts,
    dense_cot,
    advantage,
    dense_master,
    dense_first,
    dense_second,
    routed_grads,
    routed_master,
    routed_first,
    routed_second,
):
    token_total = dense_acts.shape[0] * lax.axis_size("ep") * lax.axis_size("edp")
    factor = 1.0 / math.sqrt(token_total)
    scaled = (advantage[:, None] * dense_cot.astype(jnp.float32)).astype(jnp.bfloat16)
    local_grad = (
        lax.dot_general(
            dense_acts, scaled, (((0,), (0,)), ((), ())), preferred_element_type=jnp.float32
        )
        * factor
    )
    dense_grad = lax.psum_scatter(local_grad, ("ep", "edp"), scatter_dimension=0, tiled=True)
    routed_local = routed_grads[0].astype(jnp.float32)
    routed_grad = lax.psum_scatter(routed_local, "edp", scatter_dimension=1, tiled=True)
    routed_master_new, routed_first_new, routed_second_new = adamw_update(
        routed_grad, routed_master, routed_first, routed_second
    )
    routed_weights = lax.all_gather(
        routed_master_new.astype(jnp.bfloat16), "edp", axis=1, tiled=True
    )
    dense_master_new, dense_first_new, dense_second_new = adamw_update(
        dense_grad, dense_master, dense_first, dense_second
    )
    dense_shard = dense_master_new.astype(jnp.bfloat16)
    dense_weights = lax.all_gather(dense_shard, ("ep", "edp"), axis=0, tiled=True)
    return (
        dense_master_new,
        dense_first_new,
        dense_second_new,
        dense_weights,
        routed_master_new,
        routed_first_new,
        routed_second_new,
        routed_weights,
    )


def solution(mesh):
    in_specs = (
        P(("ep", "edp"), None),
        P(("ep", "edp"), None),
        P(("ep", "edp")),
        P(("ep", "edp"), None),
        P(("ep", "edp"), None),
        P(("ep", "edp"), None),
        P("edp", "ep", None, None),
        P("ep", "edp", None),
        P("ep", "edp", None),
        P("ep", "edp", None),
    )
    out_specs = (
        P(("ep", "edp"), None),
        P(("ep", "edp"), None),
        P(("ep", "edp"), None),
        P(),
        P("ep", "edp", None),
        P("ep", "edp", None),
        P("ep", "edp", None),
        P("ep", None, None),
    )
    return jax.shard_map(
        per_device, mesh=mesh, in_specs=in_specs, out_specs=out_specs, check_vma=False
    )
```

profile of v0, /device:TPU:1, one launch (start us, length us, event | category | flops | bytes accessed | tf_op | source)
XLA Modules:
  0.0 1981.2 jit_solution(11802681939479223005)
XLA Ops:
  7.2 0.0 copy-start
  7.2 0.0 all-reduce.5.cloned.1.call-start
  7.2 1.0 copy-done
  8.3 4.7 fusion
  13.0 0.0 copy-start.1
  13.0 0.0 copy-start.5
  13.0 0.0 copy-start.6
  13.0 0.0 copy-start.7
  13.0 0.0 copy-start.2
  13.0 0.0 copy-start.3
  13.0 0.0 copy-start.4
  13.0 0.0 all-reduce.5.cloned.1.call-update
  13.1 0.0 all-reduce.7.cloned.1.call-start
  13.1 0.8 copy-done.1
  13.9 0.8 bitcast_convert_fusion
  14.7 0.0 all-reduce.7.cloned.1.call-update
  14.7 0.0 all-gather.3.cloned.1.call-start
  14.8 487.4 %all-reduce.5.cloned.1.call-done = f32[512,1536]{0,1:T(8,128)} async-done(((f32[512,1536]{0,1:T(8,128)}), f32[512,1536]{0,1:T(8,128)}) %all-reduce.5.cloned.1.call-update) | async-done | bytes 3145744
  502.2 1.4 constant_dynamic-slice_fusion
  503.6 0.3 copy.75
  503.9 0.0 copy-done.5
  503.9 0.0 copy-done.6
  503.9 0.0 copy-done.7
  503.9 0.6 convert_bitcast_fusion
  504.5 0.0 all-gather.3.cloned.1.call-update
  504.6 1.3 dynamic-slice.1
  505.8 83.9 %all-reduce.7.cloned.1.call-done = f32[4,8,2048]{2,0,1:T(4,128)} async-done(((f32[4,8,2048]{2,0,1:T(4,128)}), f32[4,8,2048]{2,0,1:T(4,128)}) %all-reduce.7.cloned.1.call-update) | async-done | bytes 262160
  589.7 0.0 copy-done.2
  589.7 0.0 copy-done.3
  589.7 0.0 copy-done.4
  589.7 1.5 fusion.5
  591.2 0.6 copy.83
  591.9 0.6 copy.84
  592.5 0.6 copy.85
  593.2 22.0 %all_gather.7 = bf16[4,8,2048]{2,0,1:T(4,128)(2,1)S(1)} all-gather(bf16[4,1,2048]{2,0,1:T(4,128)(2,1)S(1)} %get-tuple-element.48), channel_id=1, replica_groups=mesh['ep'=64,'edp'=8] {'edp'}, dimensions={1}, use_global_device_ids=true | all-gather | bytes 147456 | tf_op jit(solution)/shard_map/all_gather | solution.py:51
  615.2 0.7 copy.86
  615.9 1355.4 %all-gather.3.cloned.1.call-done = bf16[512,1,1536]{2,1,0:T(2,128)(2,1)} async-done(((bf16[1,1,1536]{2,1,0:T(2,128)(2,1)}), bf16[512,1,1536]{2,1,0:T(2,128)(2,1)}) %all-gather.3.cloned.1.call-update) | async-done | bytes 1572880 | tf_op jit(solution)/shard_map/all_gather | solution.py:58
  1971.3 3.4 copy.102
Async XLA Ops:
  7.2 1.1 copy-start
  7.2 495.0 %all-reduce.5.cloned.1.call-start = ((), (), s32[]{:S(2)}) async-start(), calls=%async_computation.1 | async-start | bytes 6291456
  13.0 0.9 copy-start.1
  13.0 490.9 %copy-start.5 = (f32[1,1536]{1,0:T(1,128)S(1)}, f32[1,1536]{1,0:T(1,128)}, u32[]{:S(2)}) copy-start(f32[1,1536]{1,0:T(1,128)} %param.13) | copy-start | bytes 18436
  13.0 490.9 %copy-start.6 = (f32[1,1536]{1,0:T(1,128)S(1)}, f32[1,1536]{1,0:T(1,128)}, u32[]{:S(2)}) copy-start(f32[1,1536]{1,0:T(1,128)} %param.15) | copy-start | bytes 18436
  13.0 490.9 %copy-start.7 = (f32[1,1536]{1,0:T(1,128)S(1)}, f32[1,1536]{1,0:T(1,128)}, u32[]{:S(2)}) copy-start(f32[1,1536]{1,0:T(1,128)} %param.14) | copy-start | bytes 18436
  13.0 576.7 %copy-start.2 = (f32[4,1,2048]{2,1,0:T(1,128)S(1)}, f32[4,1,2048]{2,1,0:T(1,128)}, u32[]{:S(2)}) copy-start(f32[4,1,2048]{2,1,0:T(1,128)} %param.17) | copy-start | bytes 98308
  13.0 576.7 %copy-start.3 = (f32[4,1,2048]{2,1,0:T(1,128)S(1)}, f32[4,1,2048]{2,1,0:T(1,128)}, u32[]{:S(2)}) copy-start(f32[4,1,2048]{2,1,0:T(1,128)} %param.19) | copy-start | bytes 98308
  13.0 576.7 %copy-start.4 = (f32[4,1,2048]{2,1,0:T(1,128)S(1)}, f32[4,1,2048]{2,1,0:T(1,128)}, u32[]{:S(2)}) copy-start(f32[4,1,2048]{2,1,0:T(1,128)} %param.18) | copy-start | bytes 98308
  13.1 576.7 %all-reduce.7.cloned.1.call-start = ((), (), s32[]{:S(2)}) async-start(), calls=%async_computation.2 | async-start | bytes 524288
  14.7 1956.6 %all-gather.3.cloned.1.call-start = ((), (), s32[]{:S(2)}) async-start(), calls=%async_computation | async-start | bytes 3151872 | tf_op jit(solution)/shard_map/all_gather | solution.py:58
Sparse Core Ops, SparseCore 0:
  13.3 488.8 all-reduce.4
  505.9 83.7 all-reduce.6
  592.0 1379.3 all-gather.2
where the time goes:
time: 1990 us; the launch traced here: 1980 us
  waiting for transfers between devices  1930 us (97%)
  blocking collectives  22 us (1%)
    all_gather x1, waiting for transfers between devices, per_device(): lax.all_gather(dense_shard, ('ep', 'edp'), axis=0, tiled=True)  1360 us
    unnamed x5, waiting for transfers between devices  571 us
  transfers between devices with their start and end apart: 3, of which 3 were waited for; matrix products, arithmetic and copies ran while one was open for 0% of the time, Pallas kernels for 0%

commit v1 on v0

v1 whole, which is shorter than its diff:
```python
import math

import jax
import jax.numpy as jnp
from jax import lax
from jax.sharding import Mesh, PartitionSpec as P

beta_one = 0.9
beta_two = 0.95
learn_rate = 0.001
decay_rate = 0.1
epsilon = 1e-08

AXES = ("xh", "z", "core", "xl", "y")
SIZES = (2, 16, 2, 2, 4)
EP = ("xh", "z", "core")
EDP = ("xl", "y")
FAR = ("xh", "z")


def adamw_update(gradient, master, first_moment, second_moment):
    first_new = beta_one * first_moment + (1.0 - beta_one) * gradient
    second_new = beta_two * second_moment + (1.0 - beta_two) * gradient * gradient
    master_new = master - learn_rate * (
        first_new / (jnp.sqrt(second_new) + epsilon) + decay_rate * master
    )
    return (master_new, first_new, second_new)


def exchange(x, axes):
    return lax.all_to_all(x, axes, 0, 0, tiled=False)


def per_device(
    dense_acts,
    dense_cot,
    advantage,
    dense_master,
    dense_first,
    dense_second,
    routed_grads,
    routed_master,
    routed_first,
    routed_second,
):
    f32, bf16 = jnp.float32, jnp.bfloat16
    rows, columns = dense_acts.shape[1], dense_cot.shape[1]
    n_far, n_edp, n_core = 32, 8, 2
    half = rows // 2
    factor = 1.0 / math.sqrt(dense_acts.shape[0] * 512)
    core = lax.axis_index("core")

    packed = jnp.arange(rows)[None, :]
    which, e, far = packed // half, packed // n_far % n_edp, packed % n_far
    row = (far * n_core + jnp.where(which == 1, core, 1 - core)) * n_edp + e
    place = (jnp.arange(rows)[:, None] == row).astype(bf16)

    acts = lax.dot_general(
        dense_acts, place, (((1,), (0,)), ((), ())), preferred_element_type=bf16
    )
    scaled = (advantage[:, None] * dense_cot.astype(f32)).astype(bf16)

    def product(a):
        return lax.dot_general(a, scaled, (((0,), (0,)), ((), ())), preferred_element_type=f32)

    other = product(acts[:, :half]).astype(bf16)
    received = lax.ppermute(other, "core", [(0, 1), (1, 0)])
    own = product(acts[:, half:])
    summed = (own + received.astype(f32)).astype(bf16).reshape(n_edp, n_far, columns)

    w = 512
    routed = routed_grads[0].transpose(1, 0, 2)
    packs = [summed[:, :, i * w : (i + 1) * w] for i in range(columns // w)]
    packs += [routed[:, :, i * w : (i + 1) * w] for i in range(routed.shape[2] // w)]
    got = exchange(jnp.concatenate(packs, axis=1), EDP)
    total = jnp.sum(got, axis=0, dtype=f32)
    nd = columns // w
    dense_part = jnp.concatenate([total[i * n_far : (i + 1) * n_far] for i in range(nd)], axis=1)
    base = nd * n_far
    routed_grad = jnp.concatenate(
        [total[base + i * 4 : base + (i + 1) * 4] for i in range(routed.shape[2] // w)], axis=1
    )[:, None, :]

    got = exchange(dense_part, FAR)
    dense_grad = jnp.sum(got, axis=0, keepdims=True) * factor
    dense_master_new, dense_first_new, dense_second_new = adamw_update(
        dense_grad, dense_master, dense_first, dense_second
    )
    shard = dense_master_new.astype(bf16)
    routed_master_new, routed_first_new, routed_second_new = adamw_update(
        routed_grad, routed_master, routed_first, routed_second
    )
    shards = exchange(jnp.broadcast_to(shard, (n_far, columns)), FAR)
    rw = routed_master_new.astype(bf16)[:, 0, :]
    mine = jnp.concatenate(
        [shards[:, i * w : (i + 1) * w] for i in range(nd)]
        + [rw[:, i * w : (i + 1) * w] for i in range(routed.shape[2] // w)],
        axis=0,
    )
    got = exchange(jnp.broadcast_to(mine[None], (n_edp,) + mine.shape), EDP)
    own_w = jnp.concatenate([got[:, i * n_far : (i + 1) * n_far] for i in range(nd)], axis=2)
    own_w = own_w.reshape(half, columns)
    other_w = lax.ppermute(own_w, "core", [(0, 1), (1, 0)])
    routed_weights = jnp.concatenate(
        [got[:, base + i * 4 : base + (i + 1) * 4] for i in range(routed.shape[2] // w)], axis=2
    ).transpose(1, 0, 2)
    dense_weights = lax.dot_general(
        place[:, half:], own_w, (((1,), (0,)), ((), ())), preferred_element_type=f32
    ) + lax.dot_general(
        place[:, :half], other_w, (((1,), (0,)), ((), ())), preferred_element_type=f32
    )
    return (
        dense_master_new,
        dense_first_new,
        dense_second_new,
        dense_weights.astype(bf16),
        routed_master_new,
        routed_first_new,
        routed_second_new,
        routed_weights,
    )


def solution(mesh):
    inner = Mesh(mesh.devices.reshape(SIZES), AXES)
    in_specs = (
        P(AXES, None),
        P(AXES, None),
        P(AXES),
        P(AXES, None),
        P(AXES, None),
        P(AXES, None),
        P(EDP, EP, None, None),
        P(EP, EDP, None),
        P(EP, EDP, None),
        P(EP, EDP, None),
    )
    out_specs = (
        P(AXES, None),
        P(AXES, None),
        P(AXES, None),
        P(),
        P(EP, EDP, None),
        P(EP, EDP, None),
        P(EP, EDP, None),
        P(EP, None, None),
    )
    return jax.shard_map(
        per_device, mesh=inner, in_specs=in_specs, out_specs=out_specs, check_vma=False
    )
```

time: 1990 us -> 116 us (0.06)
  waiting for transfers between devices: 1930 us -> 34.9 us
  starting transfers between devices: 0.12 us -> 35.4 us
    all_gather x1 -> x0, waiting for transfers between devices: 1360 us -> none  [per_device(): lax.all_gather(dense_shard, ('ep', 'edp'), axis=0, tiled=True)]
    unnamed x5 -> x0, waiting for transfers between devices: 571 us -> none
    all_to_all x0 -> x2, waiting for transfers between devices: none -> 33.1 us  [exchange(): return lax.all_to_all(x, axes, 0, 0, tiled=False)]
    all_to_all x0 -> x2, blocking collectives: none -> 28.8 us  [exchange(): return lax.all_to_all(x, axes, 0, 0, tiled=False)]
    all_gather x1 -> x0, blocking collectives: 22 us -> none  [per_device(): lax.all_gather(routed_master_new.astype(jnp.bfloat16), 'edp', axis=1, til...]
  transfers between devices with their start and end apart: 3 -> 4, of which waited for: 3 -> 3; matrix products, arithmetic and copies ran while one was open for 0% -> 3% of each run, Pallas kernels for 0% -> 0%
where the time goes in v1:
time: 116 us
  starting transfers between devices  35.4 us (31%)
  waiting for transfers between devices  34.9 us (30%)
  blocking collectives  28.8 us (25%)
  local copies, waits for them, and re-layouts  6.86 us (6%)
  matrix products  6.41 us (6%)
  other arithmetic  2.52 us (2%)
    all_to_all x2, waiting for transfers between devices, exchange(): return lax.all_to_all(x, axes, 0, 0, tiled=False)  33.1 us
    all_to_all x2, blocking collectives, exchange(): return lax.all_to_all(x, axes, 0, 0, tiled=False)  28.8 us
    all_to_all x2, starting transfers between devices, exchange(): return lax.all_to_all(x, axes, 0, 0, tiled=False)  19.5 us
    ppermute x1, starting transfers between devices, per_device(): received = lax.ppermute(other, 'core', [(0, 1), (1, 0)])  8.8 us
    ppermute x1, starting transfers between devices, per_device(): other_w = lax.ppermute(own_w, 'core', [(0, 1), (1, 0)])  7.02 us
    unnamed x27, local copies, waits for them, and re-layouts  4.55 us
    dot_general x2, matrix products, product(): lax.dot_general(a, scaled, (((0,), (0,)), ((), ())), preferred_element_ty...  3.49 us
  transfers between devices with their start and end apart: 4, of which 3 were waited for; matrix products, arithmetic and copies ran while one was open for 3% of the time, Pallas kernels for 0%

profile of v1, /device:TPU:1, one launch (start us, length us, event | category | flops | bytes accessed | tf_op | source)
XLA Modules:
  0.0 115.8 jit_solution(12155719916392310331)
XLA Ops:
  0.6 0.0 copy-start
  0.7 1.1 copy-done
  1.7 0.6 fusion.1
  2.3 0.0 copy-start.1
  2.4 0.0 copy-start.8
  2.4 0.0 copy-start.9
  2.4 2.6 %convolution_convert_fusion = bf16[256,1536]{1,0:T(8,128)(2,1)S(1)} fusion(bf16[640,1536]{1,0:T(8,128)(2,1)} %param.11, f32[640]{0:T(1024)} %param.12, bf16[640,512]{0,1:T(8,128)(2,1)S(1)} %fusion.1), kind=kOutput, calls=%fused_computation.3 | convolution fusion | flops 506658816 | bytes 3082752 | tf_op jit(solution)/shard_map/dot_general | solution.py:64
  5.0 8.8 %collective-permute-start = (bf16[256,1536]{1,0:T(8,128)(2,1)S(1)}, bf16[256,1536]{1,0:T(8,128)(2,1)S(1)}, u32[]{:S(2)}, u32[]{:S(2)}) collective-permute-start(bf16[256,1536]{1,0:T(8,128)(2,1)S(1)} %convolution_convert_fusion), channel_id=1, source_target_pairs={{0,8},{8,0},{1,9},{9,1},{2,10},{10,2},{3,11},{11,3},{4,12},{12,4},... | collective-permute-start | bytes 2359304 | tf_op jit(solution)/shard_map/ppermute | solution.py:67
  13.8 0.0 copy-done.1
  13.9 1.8 %collective-permute-done = bf16[256,1536]{1,0:T(8,128)(2,1)S(1)} collective-permute-done((bf16[256,1536]{1,0:T(8,128)(2,1)S(1)}, bf16[256,1536]{1,0:T(8,128)(2,1)S(1)}, u32[]{:S(2)}, u32[]{:S(2)}) %collective-permute-start) | collective-permute-done | bytes 786464 | tf_op jit(solution)/shard_map/ppermute | solution.py:67
  15.7 0.0 copy-done.8
  15.7 0.0 copy-done.9
  15.7 0.9 add_convert_fusion
  16.6 0.1 fusion.27
  16.7 0.4 concatenate.46
  17.0 16.0 %all_to_all.28 = bf16[8,112,512]{2,1,0:T(8,128)(2,1)S(1)} all-to-all(bf16[8,112,512]{2,1,0:T(8,128)(2,1)S(1)} %concatenate.46), channel_id=1, replica_groups=mesh['xh'=2,'z'=16,'core'=2,'xl'=2,'y'=4] {'xl','y'}, dimensions={0} | all-to-all | bytes 1835008 | tf_op jit(solution)/shard_map/all_to_all | solution.py:31
  33.0 0.0 copy-start.5
  33.0 0.0 copy-start.6
  33.0 0.0 copy-start.7
  33.0 0.0 copy-start.2
  33.0 0.0 copy-start.3
  33.0 0.0 copy-start.4
  33.0 0.1 convert_reduce_fusion
  33.2 0.9 copy.49
  34.1 14.3 %all-to-all-start.1 = ((f32[32,1,1536]{2,1,0:T(1,128)}), f32[32,1,1536]{2,1,0:T(1,128)S(1)}, u32[]{:S(2)}, u32[]{:S(2)}) async-start(f32[32,1,1536]{2,1,0:T(1,128)} %copy.49), calls=%async_computation.1 | async-start | bytes 393216 | tf_op jit(solution)/shard_map/all_to_all | solution.py:31
  48.4 17.9 %all-to-all-done.1 = f32[32,1,1536]{2,1,0:T(1,128)S(1)} async-done(((f32[32,1,1536]{2,1,0:T(1,128)}), f32[32,1,1536]{2,1,0:T(1,128)S(1)}, u32[]{:S(2)}, u32[]{:S(2)}) %all-to-all-start.1) | async-done | bytes 196640 | tf_op jit(solution)/shard_map/all_to_all | solution.py:31
  66.3 0.1 reduce_sum.19
  66.5 0.0 copy-done.5
  66.5 0.0 copy-done.6
  66.5 0.0 copy-done.7
  66.5 0.6 convert_reduce_fusion.1
  67.2 0.1 broadcast_in_dim.14
  67.3 0.5 broadcast.218
  67.8 1.2 %reduce.3 = bf16[32,1536]{1,0:T(8,128)(2,1)S(1)} reduce(bf16[32,1,1536]{2,1,0:T(2,128)(2,1)S(1)} %broadcast_in_dim.14, bf16[]{:T(256)} %broadcast.218), dimensions={1}, to_apply=%broadcast_in_dim.14.reduce_sub_computation | reduce | bytes 196610 | tf_op jit(solution)/shard_map/broadcast_in_dim | solution.py:93
  69.0 0.7 reshape.341
  69.7 5.2 %all-to-all-start.2 = ((bf16[32,2,768]{2,1,0:T(2,128)(2,1)}), bf16[32,2,768]{2,1,0:T(2,128)(2,1)S(1)}, u32[]{:S(2)}, u32[]{:S(2)}) async-start(bf16[32,2,768]{2,1,0:T(2,128)(2,1)} %reshape.341), calls=%async_computation.2 | async-start | bytes 196608 | tf_op jit(solution)/shard_map/all_to_all | solution.py:31
  74.9 0.0 copy-done.2
  74.9 0.0 copy-done.3
  74.9 0.0 copy-done.4
  74.9 0.1 convert_bitcast_fusion
  75.0 15.2 %all-to-all-done.2 = bf16[32,2,768]{2,1,0:T(2,128)(2,1)S(1)} async-done(((bf16[32,2,768]{2,1,0:T(2,128)(2,1)}), bf16[32,2,768]{2,1,0:T(2,128)(2,1)S(1)}, u32[]{:S(2)}, u32[]{:S(2)}) %all-to-all-start.2) | async-done | bytes 98336 | tf_op jit(solution)/shard_map/all_to_all | solution.py:31
  90.3 0.1 reshape.342
  90.4 0.1 concatenate.53
  90.4 0.1 broadcast_in_dim.15
  90.5 12.8 %all_to_all.29 = bf16[8,112,512]{2,1,0:T(8,128)(2,1)S(1)} all-to-all(bf16[8,112,512]{2,1,0:T(8,128)(2,1)S(1)} %broadcast_in_dim.15), channel_id=1, replica_groups=mesh['xh'=2,'z'=16,'core'=2,'xl'=2,'y'=4] {'xl','y'}, dimensions={0} | all-to-all | bytes 1835008 | tf_op jit(solution)/shard_map/all_to_all | solution.py:31
  103.4 0.1 fusion.26
  103.4 0.1 pad_maximum_fusion
  103.5 7.0 %collective-permute-start.1 = (bf16[256,1536]{1,0:T(8,128)(2,1)S(1)}, bf16[256,1536]{1,0:T(8,128)(2,1)S(1)}, u32[]{:S(2)}, u32[]{:S(2)}) collective-permute-start(bf16[256,1536]{1,0:T(8,128)(2,1)S(1)} %bitcast.27), channel_id=1, source_target_pairs={{0,8},{8,0},{1,9},{9,1},{2,10},{10,2},{3,11},{11,3},{4,12},{12,4},... | collective-permute-start | bytes 2359304 | tf_op jit(solution)/shard_map/ppermute | solution.py:103
  110.5 0.2 iota_compare_fusion
  110.7 0.6 copy.54
  111.3 0.6 copy.56
  112.0 0.6 copy.55
  112.7 0.1 maximum_bitcast_fusion.1
  112.7 0.7 copy.57
  113.5 0.6 fusion.5
  114.1 0.0 collective-permute-done.1
  114.1 1.7 %fusion = bf16[512,1536]{1,0:T(8,128)(2,1)} fusion(f32[512,1536]{1,0:T(8,128)S(1)} %fusion.5, bf16[256,1536]{1,0:T(8,128)(2,1)S(1)} %collective-permute-done.1, pred[512,512]{1,0:T(32,128)(4,1)S(1)} %iota_compare_fusion), kind=kOutput, calls=%fused_computation.2 | convolution fusion | flops 404226048 | bytes 5636096 | tf_op jit(solution)/shard_map/dot_general | solution.py:109
  (14 shorter events, 0.2 us)
Async XLA Ops:
  0.6 1.1 copy-start
  2.3 11.4 %copy-start.1 = (bf16[1,4,8,2048]{3,2,1,0:T(8,128)(2,1)S(1)}, bf16[1,4,8,2048]{3,2,1,0:T(8,128)(2,1)}, u32[]{:S(2)}) copy-start(bf16[1,4,8,2048]{3,2,1,0:T(8,128)(2,1)} %param.16) | copy-start | bytes 393220
  2.4 13.3 %copy-start.8 = (bf16[640,1536]{1,0:T(8,128)(2,1)S(1)}, bf16[640,1536]{1,0:T(8,128)(2,1)}, u32[]{:S(2)}) copy-start(bf16[640,1536]{1,0:T(8,128)(2,1)} %param.11) | copy-start | bytes 5898244
  2.4 13.3 %copy-start.9 = (f32[640]{0:T(1024)S(1)}, f32[640]{0:T(1024)}, u32[]{:S(2)}) copy-start(f32[640]{0:T(1024)} %param.12) | copy-start | bytes 7684
  5.0 10.7 %collective-permute-start = (bf16[256,1536]{1,0:T(8,128)(2,1)S(1)}, bf16[256,1536]{1,0:T(8,128)(2,1)S(1)}, u32[]{:S(2)}, u32[]{:S(2)}) collective-permute-start(bf16[256,1536]{1,0:T(8,128)(2,1)S(1)} %convolution_convert_fusion), channel_id=1, source_target_pairs={{0,8},{8,0},{1,9},{9,1},{2,10},{10,2},{3,11},{11,3},{4,12},{12,4},... | collective-permute-start | bytes 2359304 | tf_op jit(solution)/shard_map/ppermute | solution.py:67
  33.0 33.5 %copy-start.5 = (f32[1,1536]{1,0:T(1,128)S(1)}, f32[1,1536]{1,0:T(1,128)}, u32[]{:S(2)}) copy-start(f32[1,1536]{1,0:T(1,128)} %param.13) | copy-start | bytes 18436
  33.0 33.5 %copy-start.6 = (f32[1,1536]{1,0:T(1,128)S(1)}, f32[1,1536]{1,0:T(1,128)}, u32[]{:S(2)}) copy-start(f32[1,1536]{1,0:T(1,128)} %param.15) | copy-start | bytes 18436
  33.0 33.5 %copy-start.7 = (f32[1,1536]{1,0:T(1,128)S(1)}, f32[1,1536]{1,0:T(1,128)}, u32[]{:S(2)}) copy-start(f32[1,1536]{1,0:T(1,128)} %param.14) | copy-start | bytes 18436
  33.0 41.9 %copy-start.2 = (f32[4,1,2048]{2,1,0:T(1,128)S(1)}, f32[4,1,2048]{2,1,0:T(1,128)}, u32[]{:S(2)}) copy-start(f32[4,1,2048]{2,1,0:T(1,128)} %param.17) | copy-start | bytes 98308
  33.0 41.9 %copy-start.3 = (f32[4,1,2048]{2,1,0:T(1,128)S(1)}, f32[4,1,2048]{2,1,0:T(1,128)}, u32[]{:S(2)}) copy-start(f32[4,1,2048]{2,1,0:T(1,128)} %param.19) | copy-start | bytes 98308
  33.0 41.9 %copy-start.4 = (f32[4,1,2048]{2,1,0:T(1,128)S(1)}, f32[4,1,2048]{2,1,0:T(1,128)}, u32[]{:S(2)}) copy-start(f32[4,1,2048]{2,1,0:T(1,128)} %param.18) | copy-start | bytes 98308
  34.1 32.2 %all-to-all-start.1 = ((f32[32,1,1536]{2,1,0:T(1,128)}), f32[32,1,1536]{2,1,0:T(1,128)S(1)}, u32[]{:S(2)}, u32[]{:S(2)}) async-start(f32[32,1,1536]{2,1,0:T(1,128)} %copy.49), calls=%async_computation.1 | async-start | bytes 393216 | tf_op jit(solution)/shard_map/all_to_all | solution.py:31
  69.7 20.6 %all-to-all-start.2 = ((bf16[32,2,768]{2,1,0:T(2,128)(2,1)}), bf16[32,2,768]{2,1,0:T(2,128)(2,1)S(1)}, u32[]{:S(2)}, u32[]{:S(2)}) async-start(bf16[32,2,768]{2,1,0:T(2,128)(2,1)} %reshape.341), calls=%async_computation.2 | async-start | bytes 196608 | tf_op jit(solution)/shard_map/all_to_all | solution.py:31
  103.5 10.6 %collective-permute-start.1 = (bf16[256,1536]{1,0:T(8,128)(2,1)S(1)}, bf16[256,1536]{1,0:T(8,128)(2,1)S(1)}, u32[]{:S(2)}, u32[]{:S(2)}) collective-permute-start(bf16[256,1536]{1,0:T(8,128)(2,1)S(1)} %bitcast.27), channel_id=1, source_target_pairs={{0,8},{8,0},{1,9},{9,1},{2,10},{10,2},{3,11},{11,3},{4,12},{12,4},... | collective-permute-start | bytes 2359304 | tf_op jit(solution)/shard_map/ppermute | solution.py:103

commit v2 on v1

v2 whole, which is shorter than its diff:
```python
import math

import jax
import jax.numpy as jnp
from jax import lax
from jax.experimental import pallas as pl
from jax.experimental.pallas import tpu as pltpu
from jax.sharding import Mesh, PartitionSpec as P

beta_one = 0.9
beta_two = 0.95
learn_rate = 0.001
decay_rate = 0.1
epsilon = 1e-08

AXES = ("xh", "z", "core", "xl", "y")
SIZES = (2, 16, 2, 2, 4)
EP = ("xh", "z", "core")
EDP = ("xl", "y")
NEAR = ("xh", "xl", "y")
FAR = ("z",)
N_NEAR, N_FAR, N_EDP, N_CORE, N_XH, N_DEV = 16, 16, 8, 2, 2, 512
ROWS, COLUMNS, EXPERTS, FF = 512, 1536, 4, 2048
HALF = ROWS // 2
W = 512
N_DENSE, N_ROUTED = COLUMNS // W, FF // W
DENSE_ROWS = N_DENSE * N_FAR
PACKED_ROWS = DENSE_ROWS + N_ROUTED * EXPERTS
LANES = 128
PIECES = COLUMNS // LANES
PIECE_ROWS = 16
f32, bf16 = jnp.float32, jnp.bfloat16


def adamw_update(gradient, master, first_moment, second_moment):
    first_new = beta_one * first_moment + (1.0 - beta_one) * gradient
    second_new = beta_two * second_moment + (1.0 - beta_two) * gradient * gradient
    master_new = master - learn_rate * (
        first_new / (jnp.sqrt(second_new) + epsilon) + decay_rate * master
    )
    return (master_new, first_new, second_new)


def exchange(x, axes):
    return lax.all_to_all(x, axes, 0, 0, tiled=False)


def iota(shape, dim):
    return lax.broadcasted_iota(jnp.int32, shape, dim)


def call(kernel, out_shape, flops=0, nbytes=1 << 20, scratch=()):
    return pl.pallas_call(
        kernel,
        out_shape=out_shape,
        scratch_shapes=scratch,
        compiler_params=pltpu.CompilerParams(vmem_limit_bytes=24 << 20),
        cost_estimate=pl.CostEstimate(flops=flops, bytes_accessed=nbytes, transcendentals=0),
    )


def pack_kernel(own, received, routed, out):
    for i in range(N_DENSE):
        cols = slice(i * W, (i + 1) * W)
        s = own[:, cols] + received[:, cols].astype(f32)
        out[:, i * N_FAR : (i + 1) * N_FAR, :] = s.astype(bf16).reshape(N_NEAR, N_FAR, W)
    xh = lax.axis_index("xh")
    shape = (N_NEAR * 16, EXPERTS * N_EDP)
    q, c = iota(shape, 0), iota(shape, 1)
    same = (q // 128 == xh) & (q // 16 % N_EDP == c % N_EDP) & (q % EXPERTS == c // N_EDP)
    total = jnp.zeros((N_NEAR * 16, W), f32)
    for b in range(N_ROUTED):
        pick = jnp.where(same & (q // EXPERTS % N_ROUTED == b), 1.0, 0.0).astype(bf16)
        total += jnp.dot(pick, routed[:, b * W : (b + 1) * W], preferred_element_type=f32)
    out[:, DENSE_ROWS:, :] = total.astype(bf16).reshape(N_NEAR, 16, W)


def middle_kernel(got, master, first, second, far_out, master_out, first_out, second_out, weights_out):
    total = jnp.sum(got[...].astype(f32), axis=0)
    pieces = [
        total[i * N_FAR : (i + 1) * N_FAR, j * LANES : (j + 1) * LANES]
        for i in range(N_DENSE)
        for j in range(W // LANES)
    ]
    pieces += [jnp.zeros((N_FAR, LANES), f32)] * (PIECE_ROWS - PIECES)
    far_out[...] = jnp.swapaxes(jnp.stack(pieces, axis=0), 0, 1).astype(bf16)
    rows = []
    for x in range(EXPERTS):
        g = jnp.concatenate(
            [total[DENSE_ROWS + b * EXPERTS + x][None] for b in range(N_ROUTED)], axis=1
        )
        p, m, v = adamw_update(g, master[x], first[x], second[x])
        master_out[x], first_out[x], second_out[x] = p, m, v
        rows.append(p)
    packed = [rows[x][:, b * W : (b + 1) * W] for b in range(N_ROUTED) for x in range(EXPERTS)]
    weights_out[...] = jnp.concatenate(packed, axis=0).astype(bf16)


def update_kernel(factor, got, master, first, second, far_out, master_out, first_out, second_out):
    total = jnp.sum(got[...].astype(f32), axis=0)
    g = jnp.concatenate([total[k : k + 1] for k in range(PIECES)], axis=1) * factor
    p, m, v = adamw_update(g, master[...], first[...], second[...])
    master_out[...], first_out[...], second_out[...] = p, m, v
    pieces = [p[:, k * LANES : (k + 1) * LANES] for k in range(PIECES)]
    pieces += [jnp.zeros((PIECE_ROWS - PIECES, LANES), f32)]
    row = jnp.concatenate(pieces, axis=0).astype(bf16)
    far_out[...] = jnp.broadcast_to(row[None], far_out.shape)


def spread_kernel(got, weights, out):
    rows = jnp.swapaxes(got[...].astype(f32), 0, 1)
    per = W // LANES
    blocks = [
        jnp.concatenate([rows[i * per + j] for j in range(per)], axis=1) for i in range(N_DENSE)
    ]
    block = jnp.concatenate(blocks, axis=0).astype(bf16)
    for d in range(N_NEAR):
        out[d, :DENSE_ROWS, :] = block
        out[d, DENSE_ROWS:, :] = weights[...]


def unpack_kernel(own, other, dense_out, routed_out):
    core, xh = lax.axis_index("core"), lax.axis_index("xh")
    n = HALF
    r, p = iota((n, n), 0), iota((n, n), 1)
    here = r // N_EDP % N_CORE == core
    same = (r // 16 == p % N_FAR) & (r % N_EDP == p // N_FAR % N_EDP) & (here == (p < n // 2))
    place = jnp.where(same, 1.0, 0.0).astype(bf16)
    for x in range(N_XH):
        for i in range(N_DENSE):
            parts = [
                ref[x * N_EDP : (x + 1) * N_EDP, i * N_FAR : (i + 1) * N_FAR, :].reshape(n // 2, W)
                for ref in (own, other)
            ]
            block = jnp.concatenate(parts, axis=0)
            dense_out[x * n : (x + 1) * n, i * W : (i + 1) * W] = jnp.dot(
                place, block, preferred_element_type=f32
            ).astype(bf16)
    shape = (EXPERTS * N_EDP, N_NEAR * 16)
    c, q = iota(shape, 0), iota(shape, 1)
    same = (q // 128 == xh) & (q // 16 % N_EDP == c % N_EDP) & (q % EXPERTS == c // N_EDP)
    packed = own[:, DENSE_ROWS:, :].reshape(N_NEAR * 16, W)
    for b in range(N_ROUTED):
        pick = jnp.where(same & (q // EXPERTS % N_ROUTED == b), 1.0, 0.0).astype(bf16)
        routed_out[:, b * W : (b + 1) * W] = jnp.dot(
            pick, packed, preferred_element_type=f32
        ).astype(bf16)


def per_device(
    dense_acts,
    dense_cot,
    advantage,
    dense_master,
    dense_first,
    dense_second,
    routed_grads,
    routed_master,
    routed_first,
    routed_second,
):
    factor = 1.0 / math.sqrt(dense_acts.shape[0] * N_DEV)
    core = lax.axis_index("core")
    sds = jax.ShapeDtypeStruct

    packed = jnp.arange(ROWS)[None, :]
    which, xh, e, z = packed // HALF, packed // 128 % N_XH, packed // N_FAR % N_EDP, packed % N_FAR
    row = ((xh * N_FAR + z) * N_CORE + jnp.where(which == 1, core, 1 - core)) * N_EDP + e
    place = (jnp.arange(ROWS)[:, None] == row).astype(bf16)

    acts = lax.dot_general(
        dense_acts, place, (((1,), (0,)), ((), ())), preferred_element_type=bf16
    )
    scaled = (advantage[:, None] * dense_cot.astype(f32)).astype(bf16)

    def product(a):
        return lax.dot_general(a, scaled, (((0,), (0,)), ((), ())), preferred_element_type=f32)

    swap = [(0, 1), (1, 0)]
    received = lax.ppermute(product(acts[:, :HALF]).astype(bf16), "core", swap)
    own = product(acts[:, HALF:])
    near = sds((N_NEAR, PACKED_ROWS, W), bf16)
    far = sds((N_FAR, PIECE_ROWS, LANES), bf16)
    rows_r = sds((EXPERTS, 1, FF), f32)
    rows_d = sds((1, COLUMNS), f32)
    sent = call(pack_kernel, near)(own, received, routed_grads.reshape(EXPERTS * N_EDP, FF))
    got = exchange(sent, NEAR)
    far_sent, routed_master_new, routed_first_new, routed_second_new, weights = call(
        middle_kernel, (far, rows_r, rows_r, rows_r, sds((16, W), bf16))
    )(got, routed_master, routed_first, routed_second)
    got = exchange(far_sent, FAR)

    def update(*refs):
        update_kernel(factor, *refs)

    far_sent, dense_master_new, dense_first_new, dense_second_new = call(
        update, (far, rows_d, rows_d, rows_d)
    )(got, dense_master, dense_first, dense_second)
    got = exchange(far_sent, FAR)
    own = exchange(call(spread_kernel, near)(got, weights), NEAR)
    other = lax.ppermute(own, "core", swap)
    dense_weights, routed_weights = call(
        unpack_kernel, (sds((ROWS, COLUMNS), bf16), sds((EXPERTS * N_EDP, FF), bf16))
    )(own, other)
    return (
        dense_master_new,
        dense_first_new,
        dense_second_new,
        dense_weights,
        routed_master_new,
        routed_first_new,
        routed_second_new,
        routed_weights.reshape(EXPERTS, N_EDP, FF),
    )


def solution(mesh):
    inner = Mesh(mesh.devices.reshape(SIZES), AXES)
    in_specs = (
        P(AXES, None),
        P(AXES, None),
        P(AXES),
        P(AXES, None),
        P(AXES, None),
        P(AXES, None),
        P(EDP, EP, None, None),
        P(EP, EDP, None),
        P(EP, EDP, None),
        P(EP, EDP, None),
    )
    out_specs = (
        P(AXES, None),
        P(AXES, None),
        P(AXES, None),
        P(),
        P(EP, EDP, None),
        P(EP, EDP, None),
        P(EP, EDP, None),
        P(EP, None, None),
    )
    return jax.shard_map(
        per_device, mesh=inner, in_specs=in_specs, out_specs=out_specs, check_vma=False
    )
```

time: 116 us -> 104 us (0.90)
  blocking collectives: 28.8 us -> 73.2 us
  waiting for transfers between devices: 34.9 us -> 3.22 us
  starting transfers between devices: 35.4 us -> 17.2 us
  local copies, waits for them, and re-layouts: 6.86 us -> 1.11 us
  Pallas kernels: 0 us -> 3.87 us
  other arithmetic: 2.52 us -> 0.01 us
  matrix products: 6.41 us -> 4.08 us
    all_to_all x2 -> x4, blocking collectives: 28.8 us -> 73.2 us  [exchange(): return lax.all_to_all(x, axes, 0, 0, tiled=False)]
    all_to_all x2 -> x0, waiting for transfers between devices: 33.1 us -> none  [exchange(): return lax.all_to_all(x, axes, 0, 0, tiled=False)]
    all_to_all x2 -> x0, starting transfers between devices: 19.5 us -> none  [exchange(): return lax.all_to_all(x, axes, 0, 0, tiled=False)]
    pallas_call x0 -> x5, Pallas kernels: none -> 3.87 us  [the longest x1 1.78 us: per_device(): call(unpack_kernel, (sds((ROWS, COLUMNS), bf16), sds((EXPERTS * N_EDP, FF...]
    unnamed x27 -> x20, local copies, waits for them, and re-layouts: 4.55 us -> 1.11 us
    dot_general x2 -> x0, matrix products: 2.3 us -> none  [the longest x1 1.72 us: per_device(): lax.dot_general(place[:, :half], other_w, (((1,), (0,)), ((), ())), prefe...]
    ppermute x2, waiting for transfers between devices: 1.76 us -> 3.22 us  [the longest x1 2.26 us: per_device(): other = lax.ppermute(own, 'core', swap)]
    ppermute x2, starting transfers between devices: 15.8 us -> 17.2 us  [the longest x1 8.91 us: per_device(): received = lax.ppermute(product(acts[:, :HALF]).astype(bf16), 'core', swap)]
  transfers between devices with their start and end apart: 4 -> 2, of which waited for: 3 -> 2; matrix products, arithmetic and copies ran while one was open for 3% -> 1% of each run, Pallas kernels for 0% -> 0%
where the time goes in v2:
time: 104 us; the launch traced here: 103 us
  blocking collectives  73.2 us (70%)
  starting transfers between devices  17.2 us (17%)
  matrix products  4.08 us (4%)
  Pallas kernels  3.87 us (4%)
  waiting for transfers between devices  3.22 us (3%)
  local copies, waits for them, and re-layouts  1.11 us (1%)
    all_to_all x4, blocking collectives, exchange(): return lax.all_to_all(x, axes, 0, 0, tiled=False)  73.2 us
    ppermute x1, starting transfers between devices, per_device(): received = lax.ppermute(product(acts[:, :HALF]).astype(bf16), 'core', swap)  8.91 us
    ppermute x1, starting transfers between devices, per_device(): other = lax.ppermute(own, 'core', swap)  8.27 us
    dot_general x2, matrix products, product(): lax.dot_general(a, scaled, (((0,), (0,)), ((), ())), preferred_element_ty...  3.47 us
    ppermute x1, waiting for transfers between devices, per_device(): other = lax.ppermute(own, 'core', swap)  2.26 us
  transfers between devices with their start and end apart: 2, of which 2 were waited for; matrix products, arithmetic and copies ran while one was open for 1% of the time, Pallas kernels for 0%

profile of v2, /device:TPU:1, one launch (start us, length us, event | category | flops | bytes accessed | tf_op | source)
XLA Modules:
  0.0 103.4 jit_solution(5672253678092924266)
XLA Ops:
  0.6 0.0 copy-start
  0.7 1.1 %copy-done = bf16[640,512]{1,0:T(8,128)(2,1)S(1)} copy-done((bf16[640,512]{1,0:T(8,128)(2,1)S(1)}, bf16[640,512]{1,0:T(8,128)(2,1)}, u32[]{:S(2)}) %copy-start) | copy-done | bytes 655384
  1.7 0.6 fusion
  2.3 0.0 copy-start.8
  2.4 0.0 copy-start.9
  2.4 2.6 %convolution_convert_fusion = bf16[256,1536]{1,0:T(8,128)(2,1)S(1)} fusion(bf16[640,1536]{1,0:T(8,128)(2,1)} %param.11, f32[640]{0:T(1024)} %param.12, bf16[640,512]{0,1:T(8,128)(2,1)S(1)} %fusion), kind=kOutput, calls=%fused_computation.1 | convolution fusion | flops 506658816 | bytes 3082752 | tf_op jit(solution)/shard_map/dot_general | solution.py:177
  4.9 0.0 copy-start.1
  4.9 8.9 %collective-permute-start = (bf16[256,1536]{1,0:T(8,128)(2,1)S(1)}, bf16[256,1536]{1,0:T(8,128)(2,1)S(1)}, u32[]{:S(2)}, u32[]{:S(2)}) collective-permute-start(bf16[256,1536]{1,0:T(8,128)(2,1)S(1)} %convolution_convert_fusion), channel_id=1, source_target_pairs={{0,8},{8,0},{1,9},{9,1},{2,10},{10,2},{3,11},{11,3},{4,12},{12,4},... | collective-permute-start | bytes 2359304 | tf_op jit(solution)/shard_map/ppermute | solution.py:180
  13.9 0.0 copy-done.8
  13.9 0.0 copy-done.9
  13.9 0.9 fusion.2.own
  14.8 1.0 collective-permute-done.received
  15.8 0.0 copy-done.1
  15.8 0.0 copy-start.2
  15.8 0.0 copy-start.3
  15.8 0.0 copy-start.4
  15.8 0.6 shard_map.161
  16.4 0.0 copy-start.5
  16.4 0.0 copy-start.6
  16.4 0.0 copy-start.7
  16.4 18.6 %all_to_all.20.got = bf16[16,64,512]{2,1,0:T(8,128)(2,1)S(1)} all-to-all(bf16[16,64,512]{2,1,0:T(8,128)(2,1)S(1)} %shard_map.161), channel_id=1, replica_groups=mesh['xh'=2,'z'=16,'core'=2,'xl'=2,'y'=4] {'xh','xl','y'}, dimensions={0} | all-to-all | bytes 2097152 | tf_op jit(solution)/shard_map/all_to_all | solution.py:45
  35.1 0.0 copy-done.2
  35.1 0.0 copy-done.3
  35.1 0.0 copy-done.4
  35.1 0.7 shard_map.162
  35.8 25.0 %all_to_all.21.refs_0_ = bf16[16,16,128]{2,1,0:T(8,128)(2,1)S(1)} all-to-all(bf16[16,16,128]{2,1,0:T(8,128)(2,1)S(1)} %get-tuple-element.19), channel_id=1, replica_groups=mesh['xh'=2,'z'=16,'core'=2,'xl'=2,'y'=4] {'z'}, dimensions={0} | all-to-all | bytes 131072 | tf_op jit(solution)/shard_map/all_to_all | solution.py:45
  60.8 0.0 copy-done.5
  60.8 0.0 copy-done.6
  60.8 0.0 copy-done.7
  60.8 0.7 shard_map.163
  61.5 14.3 %all_to_all.22.got = bf16[16,16,128]{2,1,0:T(8,128)(2,1)S(1)} all-to-all(bf16[16,16,128]{2,1,0:T(8,128)(2,1)S(1)} %get-tuple-element.23), channel_id=1, replica_groups=mesh['xh'=2,'z'=16,'core'=2,'xl'=2,'y'=4] {'z'}, dimensions={0} | all-to-all | bytes 131072 | tf_op jit(solution)/shard_map/all_to_all | solution.py:45
  75.8 0.1 shard_map.164
  75.9 15.2 %all_to_all.23.own = bf16[16,64,512]{2,1,0:T(8,128)(2,1)S(1)} all-to-all(bf16[16,64,512]{2,1,0:T(8,128)(2,1)S(1)} %shard_map.164), channel_id=1, replica_groups=mesh['xh'=2,'z'=16,'core'=2,'xl'=2,'y'=4] {'xh','xl','y'}, dimensions={0} | all-to-all | bytes 2097152 | tf_op jit(solution)/shard_map/all_to_all | solution.py:45
  91.1 8.3 %collective-permute-start.1 = (bf16[16,64,512]{2,1,0:T(8,128)(2,1)S(1)}, bf16[16,64,512]{2,1,0:T(8,128)(2,1)S(1)}, u32[]{:S(2)}, u32[]{:S(2)}) collective-permute-start(bf16[16,64,512]{2,1,0:T(8,128)(2,1)S(1)} %all_to_all.23.own), channel_id=1, source_target_pairs={{0,8},{8,0},{1,9},{9,1},{2,10},{10,2},{3,11},{11,3},{4,12},{12,4},... | collective-permute-start | bytes 3145736 | tf_op jit(solution)/shard_map/ppermute | solution.py:201
  99.4 2.3 %collective-permute-done.1.other = bf16[16,64,512]{2,1,0:T(8,128)(2,1)S(1)} collective-permute-done((bf16[16,64,512]{2,1,0:T(8,128)(2,1)S(1)}, bf16[16,64,512]{2,1,0:T(8,128)(2,1)S(1)}, u32[]{:S(2)}, u32[]{:S(2)}) %collective-permute-start.1) | collective-permute-done | bytes 1048608 | tf_op jit(solution)/shard_map/ppermute | solution.py:201
  101.6 1.8 %shard_map.165 = (bf16[512,1536]{1,0:T(8,128)(2,1)}, bf16[32,2048]{1,0:T(8,128)(2,1)}) custom-call(bf16[16,64,512]{2,1,0:T(8,128)(2,1)S(1)} %all_to_all.23.own, bf16[16,64,512]{2,1,0:T(8,128)(2,1)S(1)} %collective-permute-done.1.other), custom_call_target="tpu_custom_call" | custom-call | bytes 1048576 | tf_op jit(solution)/shard_map/pallas_call | solution.py:202
  (1 shorter events, 0.0 us)
Async XLA Ops:
  0.6 1.1 %copy-start = (bf16[640,512]{1,0:T(8,128)(2,1)S(1)}, bf16[640,512]{1,0:T(8,128)(2,1)}, u32[]{:S(2)}) copy-start(bf16[640,512]{1,0:T(8,128)(2,1)} %param.10) | copy-start | bytes 1966084
  2.3 11.5 %copy-start.8 = (bf16[640,1536]{1,0:T(8,128)(2,1)S(1)}, bf16[640,1536]{1,0:T(8,128)(2,1)}, u32[]{:S(2)}) copy-start(bf16[640,1536]{1,0:T(8,128)(2,1)} %param.11) | copy-start | bytes 5898244
  2.4 11.5 %copy-start.9 = (f32[640]{0:T(1024)S(1)}, f32[640]{0:T(1024)}, u32[]{:S(2)}) copy-start(f32[640]{0:T(1024)} %param.12) | copy-start | bytes 7684
  4.9 10.8 %copy-start.1 = (bf16[1,4,8,2048]{3,2,1,0:T(8,128)(2,1)S(1)}, bf16[1,4,8,2048]{3,2,1,0:T(8,128)(2,1)}, u32[]{:S(2)}) copy-start(bf16[1,4,8,2048]{3,2,1,0:T(8,128)(2,1)} %param.16) | copy-start | bytes 393220
  4.9 10.8 %collective-permute-start = (bf16[256,1536]{1,0:T(8,128)(2,1)S(1)}, bf16[256,1536]{1,0:T(8,128)(2,1)S(1)}, u32[]{:S(2)}, u32[]{:S(2)}) collective-permute-start(bf16[256,1536]{1,0:T(8,128)(2,1)S(1)} %convolution_convert_fusion), channel_id=1, source_target_pairs={{0,8},{8,0},{1,9},{9,1},{2,10},{10,2},{3,11},{11,3},{4,12},{12,4},... | collective-permute-start | bytes 2359304 | tf_op jit(solution)/shard_map/ppermute | solution.py:180
  15.8 19.3 %copy-start.2 = (f32[4,1,2048]{2,1,0:T(1,128)S(1)}, f32[4,1,2048]{2,1,0:T(1,128)}, u32[]{:S(2)}) copy-start(f32[4,1,2048]{2,1,0:T(1,128)} %master.1) | copy-start | bytes 98308
  15.8 19.3 %copy-start.3 = (f32[4,1,2048]{2,1,0:T(1,128)S(1)}, f32[4,1,2048]{2,1,0:T(1,128)}, u32[]{:S(2)}) copy-start(f32[4,1,2048]{2,1,0:T(1,128)} %first.1) | copy-start | bytes 98308
  15.8 19.3 %copy-start.4 = (f32[4,1,2048]{2,1,0:T(1,128)S(1)}, f32[4,1,2048]{2,1,0:T(1,128)}, u32[]{:S(2)}) copy-start(f32[4,1,2048]{2,1,0:T(1,128)} %second.1) | copy-start | bytes 98308
  16.4 44.4 %copy-start.5 = (f32[1,1536]{1,0:T(1,128)S(1)}, f32[1,1536]{1,0:T(1,128)}, u32[]{:S(2)}) copy-start(f32[1,1536]{1,0:T(1,128)} %refs_1_.1) | copy-start | bytes 18436
  16.4 44.4 %copy-start.6 = (f32[1,1536]{1,0:T(1,128)S(1)}, f32[1,1536]{1,0:T(1,128)}, u32[]{:S(2)}) copy-start(f32[1,1536]{1,0:T(1,128)} %refs_2_.1) | copy-start | bytes 18436
  16.4 44.4 %copy-start.7 = (f32[1,1536]{1,0:T(1,128)S(1)}, f32[1,1536]{1,0:T(1,128)}, u32[]{:S(2)}) copy-start(f32[1,1536]{1,0:T(1,128)} %refs_3_.1) | copy-start | bytes 18436
  91.1 10.5 %collective-permute-start.1 = (bf16[16,64,512]{2,1,0:T(8,128)(2,1)S(1)}, bf16[16,64,512]{2,1,0:T(8,128)(2,1)S(1)}, u32[]{:S(2)}, u32[]{:S(2)}) collective-permute-start(bf16[16,64,512]{2,1,0:T(8,128)(2,1)S(1)} %all_to_all.23.own), channel_id=1, source_target_pairs={{0,8},{8,0},{1,9},{9,1},{2,10},{10,2},{3,11},{11,3},{4,12},{12,4},... | collective-permute-start | bytes 3145736 | tf_op jit(solution)/shard_map/ppermute | solution.py:201

commit v3 on v2

--- a/solution.py
+++ b/solution.py
@@ -96,15 +96,23 @@
     weights_out[...] = jnp.concatenate(packed, axis=0).astype(bf16)
 
 
-def update_kernel(factor, got, master, first, second, far_out, master_out, first_out, second_out):
+def updated(factor, got, master, first, second):
     total = jnp.sum(got[...].astype(f32), axis=0)
     g = jnp.concatenate([total[k : k + 1] for k in range(PIECES)], axis=1) * factor
-    p, m, v = adamw_update(g, master[...], first[...], second[...])
-    master_out[...], first_out[...], second_out[...] = p, m, v
+    return adamw_update(g, master[...], first[...], second[...])
+
+
+def weights_kernel(factor, got, master, first, second, far_out):
+    p = updated(factor, got, master, first, second)[0]
     pieces = [p[:, k * LANES : (k + 1) * LANES] for k in range(PIECES)]
     pieces += [jnp.zeros((PIECE_ROWS - PIECES, LANES), f32)]
     row = jnp.concatenate(pieces, axis=0).astype(bf16)
     far_out[...] = jnp.broadcast_to(row[None], far_out.shape)
+
+
+def state_kernel(factor, got, master, first, second, master_out, first_out, second_out):
+    p, m, v = updated(factor, got, master, first, second)
+    master_out[...], first_out[...], second_out[...] = p, m, v
 
 
 def spread_kernel(got, weights, out):
@@ -119,23 +127,27 @@
         out[d, DENSE_ROWS:, :] = weights[...]
 
 
-def unpack_kernel(own, other, dense_out, routed_out):
-    core, xh = lax.axis_index("core"), lax.axis_index("xh")
-    n = HALF
-    r, p = iota((n, n), 0), iota((n, n), 1)
-    here = r // N_EDP % N_CORE == core
-    same = (r // 16 == p % N_FAR) & (r % N_EDP == p // N_FAR % N_EDP) & (here == (p < n // 2))
+def place_rows(packed, core, out, blocks, sems):
+    n = N_EDP * N_FAR
+    p, q = iota((n, n), 0), iota((n, n), 1)
+    same = (p // N_EDP == q % N_FAR) & (p % N_EDP == q // N_FAR)
     place = jnp.where(same, 1.0, 0.0).astype(bf16)
+    copies = []
     for x in range(N_XH):
         for i in range(N_DENSE):
-            parts = [
-                ref[x * N_EDP : (x + 1) * N_EDP, i * N_FAR : (i + 1) * N_FAR, :].reshape(n // 2, W)
-                for ref in (own, other)
-            ]
-            block = jnp.concatenate(parts, axis=0)
-            dense_out[x * n : (x + 1) * n, i * W : (i + 1) * W] = jnp.dot(
-                place, block, preferred_element_type=f32
-            ).astype(bf16)
+            rows = packed[x * N_EDP : (x + 1) * N_EDP, i * N_FAR : (i + 1) * N_FAR, :]
+            block = jnp.dot(place, rows.reshape(n, W), preferred_element_type=f32)
+            k = x * N_DENSE + i
+            blocks[k] = block.reshape(N_FAR, N_EDP, W).astype(bf16)
+            to = out.at[pl.ds(x * N_FAR, N_FAR), core, :, pl.ds(i * W, W)]
+            copies.append(pltpu.make_async_copy(blocks.at[k], to, sems.at[k]))
+            copies[-1].start()
+    return copies
+
+
+def own_place_kernel(own, dense_out, routed_out, blocks, sems):
+    copies = place_rows(own, lax.axis_index("core"), dense_out, blocks, sems)
+    xh = lax.axis_index("xh")
     shape = (EXPERTS * N_EDP, N_NEAR * 16)
     c, q = iota(shape, 0), iota(shape, 1)
     same = (q // 128 == xh) & (q // 16 % N_EDP == c % N_EDP) & (q % EXPERTS == c // N_EDP)
@@ -145,6 +157,13 @@
         routed_out[:, b * W : (b + 1) * W] = jnp.dot(
             pick, packed, preferred_element_type=f32
         ).astype(bf16)
+    for copy in copies:
+        copy.wait()
+
+
+def other_place_kernel(other, held, dense_out, blocks, sems):
+    for copy in place_rows(other, 1 - lax.axis_index("core"), dense_out, blocks, sems):
+        copy.wait()
 
 
 def per_device(
@@ -190,18 +209,51 @@
     )(got, routed_master, routed_first, routed_second)
     got = exchange(far_sent, FAR)
 
-    def update(*refs):
-        update_kernel(factor, *refs)
-
-    far_sent, dense_master_new, dense_first_new, dense_second_new = call(
-        update, (far, rows_d, rows_d, rows_d)
-    )(got, dense_master, dense_first, dense_second)
+    def ahead(*refs):
+        weights_kernel(factor, *refs)
+
+    def state(*refs):
+        state_kernel(factor, *refs)
+
+    dense_args = (got, dense_master, dense_first, dense_second)
+    far_sent = call(ahead, far)(*dense_args)
+    dense_master_new, dense_first_new, dense_second_new = call(state, (rows_d, rows_d, rows_d))(
+        *dense_args
+    )
     got = exchange(far_sent, FAR)
-    own = exchange(call(spread_kernel, near)(got, weights), NEAR)
+    near_sent = call(spread_kernel, near)(got, weights)
+    near_sent, dense_master_new, dense_first_new, dense_second_new = lax.optimization_barrier(
+        (near_sent, dense_master_new, dense_first_new, dense_second_new)
+    )
+    own = exchange(near_sent, NEAR)
     other = lax.ppermute(own, "core", swap)
-    dense_weights, routed_weights = call(
-        unpack_kernel, (sds((ROWS, COLUMNS), bf16), sds((EXPERTS * N_EDP, FF), bf16))
-    )(own, other)
+    dense_shape = sds((ROWS // 16, N_CORE, N_EDP, COLUMNS), bf16)
+    anywhere = pl.BlockSpec(memory_space=pl.ANY)
+    vmem = pl.BlockSpec(memory_space=pltpu.VMEM)
+    n_blocks = N_XH * N_DENSE
+    place_params = dict(
+        scratch_shapes=[
+            pltpu.VMEM((n_blocks, N_FAR, N_EDP, W), bf16),
+            pltpu.SemaphoreType.DMA((n_blocks,)),
+        ],
+        compiler_params=pltpu.CompilerParams(vmem_limit_bytes=24 << 20),
+        cost_estimate=pl.CostEstimate(flops=200 << 20, bytes_accessed=2 << 20, transcendentals=0),
+    )
+    held, routed_weights = pl.pallas_call(
+        own_place_kernel,
+        in_specs=[vmem],
+        out_specs=[anywhere, vmem],
+        out_shape=(dense_shape, sds((EXPERTS * N_EDP, FF), bf16)),
+        **place_params,
+    )(own)
+    dense_weights = pl.pallas_call(
+        other_place_kernel,
+        in_specs=[vmem, anywhere],
+        out_specs=anywhere,
+        out_shape=dense_shape,
+        input_output_aliases={1: 0},
+        **place_params,
+    )(other, held).reshape(ROWS, COLUMNS)
     return (
         dense_master_new,
         dense_first_new,

time: 104 us -> 104 us (level)
  blocking collectives: 73.2 us -> 59 us
  waiting for transfers between devices: 3.22 us -> 12.4 us
  starting transfers between devices: 17.2 us -> 20.4 us
  Pallas kernels: 3.87 us -> 5.63 us
    all_to_all x4 -> x3, blocking collectives: 73.2 us -> 59 us  [exchange(): return lax.all_to_all(x, axes, 0, 0, tiled=False)]
    all_to_all x0 -> x1, waiting for transfers between devices: none -> 10.9 us  [exchange(): return lax.all_to_all(x, axes, 0, 0, tiled=False)]
    all_to_all x0 -> x1, starting transfers between devices: none -> 3.5 us  [exchange(): return lax.all_to_all(x, axes, 0, 0, tiled=False)]
    pallas_call x3 -> x5, Pallas kernels: 2.52 us -> 4.29 us  [the longest x1 1.76 us: per_device(): pl.pallas_call(own_place_kernel, in_specs=[vmem], out_specs=[anywhere, vm...]
    ppermute x1, waiting for transfers between devices: 2.26 us -> 0.5 us  [per_device(): other = lax.ppermute(own, 'core', swap)]
  transfers between devices with their start and end apart: 2 -> 3, of which waited for: 2 -> 3; matrix products, arithmetic and copies ran while one was open for 1% -> 1% of each run, Pallas kernels for 0% -> 2%
where the time goes in v3:
time: 104 us; the launch traced here: 103 us
  blocking collectives  59 us (57%)
  starting transfers between devices  20.4 us (20%)
  waiting for transfers between devices  12.4 us (12%)
  Pallas kernels  5.63 us (5%)
  matrix products  4.08 us (4%)
  local copies, waits for them, and re-layouts  1.11 us (1%)
    all_to_all x3, blocking collectives, exchange(): return lax.all_to_all(x, axes, 0, 0, tiled=False)  59 us
    all_to_all x1, waiting for transfers between devices, exchange(): return lax.all_to_all(x, axes, 0, 0, tiled=False)  10.9 us
    ppermute x1, starting transfers between devices, per_device(): received = lax.ppermute(product(acts[:, :HALF]).astype(bf16), 'core', swap)  8.91 us
    ppermute x1, starting transfers between devices, per_device(): other = lax.ppermute(own, 'core', swap)  8 us
    all_to_all x1, starting transfers between devices, exchange(): return lax.all_to_all(x, axes, 0, 0, tiled=False)  3.5 us
    dot_general x2, matrix products, product(): lax.dot_general(a, scaled, (((0,), (0,)), ((), ())), preferred_element_ty...  3.47 us
  transfers between devices with their start and end apart: 3, of which 3 were waited for; matrix products, arithmetic and copies ran while one was open for 1% of the time, Pallas kernels for 2%

profile of v3, /device:TPU:1, one launch (start us, length us, event | category | flops | bytes accessed | tf_op | source)
XLA Modules:
  0.0 103.5 jit_solution(5293642306566791738)
XLA Ops:
  0.6 0.0 copy-start
  0.7 1.1 %copy-done = bf16[640,512]{1,0:T(8,128)(2,1)S(1)} copy-done((bf16[640,512]{1,0:T(8,128)(2,1)S(1)}, bf16[640,512]{1,0:T(8,128)(2,1)}, u32[]{:S(2)}) %copy-start) | copy-done | bytes 655384
  1.7 0.6 fusion
  2.3 0.0 copy-start.8
  2.4 0.0 copy-start.9
  2.4 2.6 %convolution_convert_fusion = bf16[256,1536]{1,0:T(8,128)(2,1)S(1)} fusion(bf16[640,1536]{1,0:T(8,128)(2,1)} %param.11, f32[640]{0:T(1024)} %param.12, bf16[640,512]{0,1:T(8,128)(2,1)S(1)} %fusion), kind=kOutput, calls=%fused_computation.1 | convolution fusion | flops 506658816 | bytes 3082752 | tf_op jit(solution)/shard_map/dot_general | solution.py:196
  4.9 0.0 copy-start.1
  4.9 8.9 %collective-permute-start = (bf16[256,1536]{1,0:T(8,128)(2,1)S(1)}, bf16[256,1536]{1,0:T(8,128)(2,1)S(1)}, u32[]{:S(2)}, u32[]{:S(2)}) collective-permute-start(bf16[256,1536]{1,0:T(8,128)(2,1)S(1)} %convolution_convert_fusion), channel_id=1, source_target_pairs={{0,8},{8,0},{1,9},{9,1},{2,10},{10,2},{3,11},{11,3},{4,12},{12,4},... | collective-permute-start | bytes 2359304 | tf_op jit(solution)/shard_map/ppermute | solution.py:199
  13.9 0.0 copy-done.8
  13.9 0.0 copy-done.9
  13.9 0.9 fusion.2.own
  14.8 1.0 collective-permute-done.received
  15.8 0.0 copy-done.1
  15.8 0.0 copy-start.2
  15.8 0.0 copy-start.3
  15.8 0.0 copy-start.4
  15.8 0.6 shard_map.161
  16.4 0.0 copy-start.5
  16.4 0.0 copy-start.6
  16.4 0.0 copy-start.7
  16.4 18.6 %all_to_all.20.got = bf16[16,64,512]{2,1,0:T(8,128)(2,1)S(1)} all-to-all(bf16[16,64,512]{2,1,0:T(8,128)(2,1)S(1)} %shard_map.161), channel_id=1, replica_groups=mesh['xh'=2,'z'=16,'core'=2,'xl'=2,'y'=4] {'xh','xl','y'}, dimensions={0} | all-to-all | bytes 2097152 | tf_op jit(solution)/shard_map/all_to_all | solution.py:45
  35.1 0.0 copy-done.2
  35.1 0.0 copy-done.3
  35.1 0.0 copy-done.4
  35.1 0.7 shard_map.162
  35.8 25.0 %all_to_all.21.refs_0_ = bf16[16,16,128]{2,1,0:T(8,128)(2,1)S(1)} all-to-all(bf16[16,16,128]{2,1,0:T(8,128)(2,1)S(1)} %get-tuple-element.22), channel_id=1, replica_groups=mesh['xh'=2,'z'=16,'core'=2,'xl'=2,'y'=4] {'z'}, dimensions={0} | all-to-all | bytes 131072 | tf_op jit(solution)/shard_map/all_to_all | solution.py:45
  60.8 0.0 copy-done.5
  60.8 0.0 copy-done.6
  60.8 0.0 copy-done.7
  60.8 0.7 shard_map.163
  61.5 3.5 %all-to-all-start.2 = ((bf16[16,16,128]{2,1,0:T(8,128)(2,1)}), bf16[16,16,128]{2,1,0:T(8,128)(2,1)S(1)}, u32[]{:S(2)}, u32[]{:S(2)}) async-start(bf16[16,16,128]{2,1,0:T(8,128)(2,1)} %shard_map.163), calls=%async_computation.2 | async-start | bytes 131072 | tf_op jit(solution)/shard_map/all_to_all | solution.py:45
  65.0 0.7 shard_map.165
  65.7 10.9 %all-to-all-done.2.got = bf16[16,16,128]{2,1,0:T(8,128)(2,1)S(1)} async-done(((bf16[16,16,128]{2,1,0:T(8,128)(2,1)}), bf16[16,16,128]{2,1,0:T(8,128)(2,1)S(1)}, u32[]{:S(2)}, u32[]{:S(2)}) %all-to-all-start.2) | async-done | bytes 65568 | tf_op jit(solution)/shard_map/all_to_all | solution.py:45
  76.6 0.1 shard_map.164
  76.7 15.4 %all_to_all.22.own = bf16[16,64,512]{2,1,0:T(8,128)(2,1)S(1)} all-to-all(bf16[16,64,512]{2,1,0:T(8,128)(2,1)S(1)} %shard_map.164), channel_id=1, replica_groups=mesh['xh'=2,'z'=16,'core'=2,'xl'=2,'y'=4] {'xh','xl','y'}, dimensions={0} | all-to-all | bytes 2097152 | tf_op jit(solution)/shard_map/all_to_all | solution.py:45
  92.1 8.0 %collective-permute-start.1 = (bf16[16,64,512]{2,1,0:T(8,128)(2,1)S(1)}, bf16[16,64,512]{2,1,0:T(8,128)(2,1)S(1)}, u32[]{:S(2)}, u32[]{:S(2)}) collective-permute-start(bf16[16,64,512]{2,1,0:T(8,128)(2,1)S(1)} %all_to_all.22.own), channel_id=1, source_target_pairs={{0,8},{8,0},{1,9},{9,1},{2,10},{10,2},{3,11},{11,3},{4,12},{12,4},... | collective-permute-start | bytes 3145736 | tf_op jit(solution)/shard_map/ppermute | solution.py:229
  100.1 1.8 %shard_map.166 = (bf16[32,2,8,1536]{3,2,1,0:T(8,128)(2,1)}, bf16[32,2048]{1,0:T(8,128)(2,1)}) custom-call(bf16[16,64,512]{2,1,0:T(8,128)(2,1)S(1)} %all_to_all.22.own), custom_call_target="tpu_custom_call" | custom-call | flops 209715200 | bytes 2097152 | tf_op jit(solution)/shard_map/pallas_call | solution.py:242
  101.9 0.5 collective-permute-done.1.other
  102.4 1.1 %shard_map.167 = bf16[32,2,8,1536]{3,2,1,0:T(8,128)(2,1)} custom-call(bf16[16,64,512]{2,1,0:T(8,128)(2,1)S(1)} %collective-permute-done.1.other, bf16[32,2,8,1536]{3,2,1,0:T(8,128)(2,1)} %get-tuple-element.31.held), custom_call_target="tpu_custom_call", output_to_operand_aliasing={{}: (1, {})} | custom-call | flops 209715200 | bytes 2097152 | tf_op jit(solution)/shard_map/pallas_call | solution.py:249
  (1 shorter events, 0.0 us)
Async XLA Ops:
  0.6 1.1 %copy-start = (bf16[640,512]{1,0:T(8,128)(2,1)S(1)}, bf16[640,512]{1,0:T(8,128)(2,1)}, u32[]{:S(2)}) copy-start(bf16[640,512]{1,0:T(8,128)(2,1)} %param.10) | copy-start | bytes 1966084
  2.3 11.5 %copy-start.8 = (bf16[640,1536]{1,0:T(8,128)(2,1)S(1)}, bf16[640,1536]{1,0:T(8,128)(2,1)}, u32[]{:S(2)}) copy-start(bf16[640,1536]{1,0:T(8,128)(2,1)} %param.11) | copy-start | bytes 5898244
  2.4 11.5 %copy-start.9 = (f32[640]{0:T(1024)S(1)}, f32[640]{0:T(1024)}, u32[]{:S(2)}) copy-start(f32[640]{0:T(1024)} %param.12) | copy-start | bytes 7684
  4.9 10.8 %copy-start.1 = (bf16[1,4,8,2048]{3,2,1,0:T(8,128)(2,1)S(1)}, bf16[1,4,8,2048]{3,2,1,0:T(8,128)(2,1)}, u32[]{:S(2)}) copy-start(bf16[1,4,8,2048]{3,2,1,0:T(8,128)(2,1)} %param.16) | copy-start | bytes 393220
  4.9 10.8 %collective-permute-start = (bf16[256,1536]{1,0:T(8,128)(2,1)S(1)}, bf16[256,1536]{1,0:T(8,128)(2,1)S(1)}, u32[]{:S(2)}, u32[]{:S(2)}) collective-permute-start(bf16[256,1536]{1,0:T(8,128)(2,1)S(1)} %convolution_convert_fusion), channel_id=1, source_target_pairs={{0,8},{8,0},{1,9},{9,1},{2,10},{10,2},{3,11},{11,3},{4,12},{12,4},... | collective-permute-start | bytes 2359304 | tf_op jit(solution)/shard_map/ppermute | solution.py:199
  15.8 19.3 %copy-start.2 = (f32[4,1,2048]{2,1,0:T(1,128)S(1)}, f32[4,1,2048]{2,1,0:T(1,128)}, u32[]{:S(2)}) copy-start(f32[4,1,2048]{2,1,0:T(1,128)} %master.1) | copy-start | bytes 98308
  15.8 19.3 %copy-start.3 = (f32[4,1,2048]{2,1,0:T(1,128)S(1)}, f32[4,1,2048]{2,1,0:T(1,128)}, u32[]{:S(2)}) copy-start(f32[4,1,2048]{2,1,0:T(1,128)} %first.1) | copy-start | bytes 98308
  15.8 19.3 %copy-start.4 = (f32[4,1,2048]{2,1,0:T(1,128)S(1)}, f32[4,1,2048]{2,1,0:T(1,128)}, u32[]{:S(2)}) copy-start(f32[4,1,2048]{2,1,0:T(1,128)} %second.1) | copy-start | bytes 98308
  16.4 44.4 %copy-start.5 = (f32[1,1536]{1,0:T(1,128)S(1)}, f32[1,1536]{1,0:T(1,128)}, u32[]{:S(2)}) copy-start(f32[1,1536]{1,0:T(1,128)} %refs_1_.3) | copy-start | bytes 18436
  16.4 44.4 %copy-start.6 = (f32[1,1536]{1,0:T(1,128)S(1)}, f32[1,1536]{1,0:T(1,128)}, u32[]{:S(2)}) copy-start(f32[1,1536]{1,0:T(1,128)} %refs_2_.3) | copy-start | bytes 18436
  16.4 44.4 %copy-start.7 = (f32[1,1536]{1,0:T(1,128)S(1)}, f32[1,1536]{1,0:T(1,128)}, u32[]{:S(2)}) copy-start(f32[1,1536]{1,0:T(1,128)} %refs_3_.3) | copy-start | bytes 18436
  61.5 15.1 %all-to-all-start.2 = ((bf16[16,16,128]{2,1,0:T(8,128)(2,1)}), bf16[16,16,128]{2,1,0:T(8,128)(2,1)S(1)}, u32[]{:S(2)}, u32[]{:S(2)}) async-start(bf16[16,16,128]{2,1,0:T(8,128)(2,1)} %shard_map.163), calls=%async_computation.2 | async-start | bytes 131072 | tf_op jit(solution)/shard_map/all_to_all | solution.py:45
  92.1 10.3 %collective-permute-start.1 = (bf16[16,64,512]{2,1,0:T(8,128)(2,1)S(1)}, bf16[16,64,512]{2,1,0:T(8,128)(2,1)S(1)}, u32[]{:S(2)}, u32[]{:S(2)}) collective-permute-start(bf16[16,64,512]{2,1,0:T(8,128)(2,1)S(1)} %all_to_all.22.own), channel_id=1, source_target_pairs={{0,8},{8,0},{1,9},{9,1},{2,10},{10,2},{3,11},{11,3},{4,12},{12,4},... | collective-permute-start | bytes 3145736 | tf_op jit(solution)/shard_map/ppermute | solution.py:229

commit v4 on v3

--- a/solution.py
+++ b/solution.py
@@ -59,11 +59,7 @@
     )
 
 
-def pack_kernel(own, received, routed, out):
-    for i in range(N_DENSE):
-        cols = slice(i * W, (i + 1) * W)
-        s = own[:, cols] + received[:, cols].astype(f32)
-        out[:, i * N_FAR : (i + 1) * N_FAR, :] = s.astype(bf16).reshape(N_NEAR, N_FAR, W)
+def routed_pack_kernel(routed, out):
     xh = lax.axis_index("xh")
     shape = (N_NEAR * 16, EXPERTS * N_EDP)
     q, c = iota(shape, 0), iota(shape, 1)
@@ -72,10 +68,18 @@
     for b in range(N_ROUTED):
         pick = jnp.where(same & (q // EXPERTS % N_ROUTED == b), 1.0, 0.0).astype(bf16)
         total += jnp.dot(pick, routed[:, b * W : (b + 1) * W], preferred_element_type=f32)
-    out[:, DENSE_ROWS:, :] = total.astype(bf16).reshape(N_NEAR, 16, W)
-
-
-def middle_kernel(got, master, first, second, far_out, master_out, first_out, second_out, weights_out):
+    out[...] = total.astype(bf16).reshape(N_NEAR, 16, W)
+
+
+def pack_kernel(own, received, routed, out):
+    for i in range(N_DENSE):
+        cols = slice(i * W, (i + 1) * W)
+        s = own[:, cols] + received[:, cols].astype(f32)
+        out[:, i * N_FAR : (i + 1) * N_FAR, :] = s.astype(bf16).reshape(N_NEAR, N_FAR, W)
+    out[:, DENSE_ROWS:, :] = routed[...]
+
+
+def middle_kernel(got, master, first, second, far_out, weights_out, routed_out):
     total = jnp.sum(got[...].astype(f32), axis=0)
     pieces = [
         total[i * N_FAR : (i + 1) * N_FAR, j * LANES : (j + 1) * LANES]
@@ -84,16 +88,17 @@
     ]
     pieces += [jnp.zeros((N_FAR, LANES), f32)] * (PIECE_ROWS - PIECES)
     far_out[...] = jnp.swapaxes(jnp.stack(pieces, axis=0), 0, 1).astype(bf16)
-    rows = []
-    for x in range(EXPERTS):
-        g = jnp.concatenate(
-            [total[DENSE_ROWS + b * EXPERTS + x][None] for b in range(N_ROUTED)], axis=1
-        )
-        p, m, v = adamw_update(g, master[x], first[x], second[x])
-        master_out[x], first_out[x], second_out[x] = p, m, v
-        rows.append(p)
+    routed = total[DENSE_ROWS:]
+    routed_out[...] = routed
+    rows = [adamw_update(routed_row(routed, x), master[x], first[x], second[x])[0] for x in range(EXPERTS)]
     packed = [rows[x][:, b * W : (b + 1) * W] for b in range(N_ROUTED) for x in range(EXPERTS)]
     weights_out[...] = jnp.concatenate(packed, axis=0).astype(bf16)
+
+
+def routed_row(routed, x):
+    return jnp.concatenate(
+        [routed[b * EXPERTS + x : b * EXPERTS + x + 1] for b in range(N_ROUTED)], axis=1
+    )
 
 
 def updated(factor, got, master, first, second):
@@ -110,9 +115,16 @@
     far_out[...] = jnp.broadcast_to(row[None], far_out.shape)
 
 
-def state_kernel(factor, got, master, first, second, master_out, first_out, second_out):
+def state_kernel(factor, got, master, first, second, routed, routed_master, routed_first, routed_second, *outs):
+    master_out, first_out, second_out, routed_master_out, routed_first_out, routed_second_out = outs
     p, m, v = updated(factor, got, master, first, second)
     master_out[...], first_out[...], second_out[...] = p, m, v
+    total = routed[...]
+    for x in range(EXPERTS):
+        p, m, v = adamw_update(
+            routed_row(total, x), routed_master[x], routed_first[x], routed_second[x]
+        )
+        routed_master_out[x], routed_first_out[x], routed_second_out[x] = p, m, v
 
 
 def spread_kernel(got, weights, out):
@@ -127,11 +139,16 @@
         out[d, DENSE_ROWS:, :] = weights[...]
 
 
-def place_rows(packed, core, out, blocks, sems):
+def place_matrix():
     n = N_EDP * N_FAR
     p, q = iota((n, n), 0), iota((n, n), 1)
     same = (p // N_EDP == q % N_FAR) & (p % N_EDP == q // N_FAR)
-    place = jnp.where(same, 1.0, 0.0).astype(bf16)
+    return jnp.where(same, 1.0, 0.0).astype(bf16)
+
+
+def place_rows(packed, core, out, blocks, sems):
+    n = N_EDP * N_FAR
+    place = place_matrix()
     copies = []
     for x in range(N_XH):
         for i in range(N_DENSE):
@@ -145,8 +162,16 @@
     return copies
 
 
-def own_place_kernel(own, dense_out, routed_out, blocks, sems):
-    copies = place_rows(own, lax.axis_index("core"), dense_out, blocks, sems)
+def own_place_kernel(core, own, dense_out, routed_out):
+    n = N_EDP * N_FAR
+    place = place_matrix()
+    for x in range(N_XH):
+        for i in range(N_DENSE):
+            rows = own[x * N_EDP : (x + 1) * N_EDP, i * N_FAR : (i + 1) * N_FAR, :]
+            block = jnp.dot(place, rows.reshape(n, W), preferred_element_type=f32)
+            dense_out[x * N_FAR : (x + 1) * N_FAR, 0, :, i * W : (i + 1) * W] = block.reshape(
+                N_FAR, N_EDP, W
+            ).astype(bf16)
     xh = lax.axis_index("xh")
     shape = (EXPERTS * N_EDP, N_NEAR * 16)
     c, q = iota(shape, 0), iota(shape, 1)
@@ -157,8 +182,6 @@
         routed_out[:, b * W : (b + 1) * W] = jnp.dot(
             pick, packed, preferred_element_type=f32
         ).astype(bf16)
-    for copy in copies:
-        copy.wait()
 
 
 def other_place_kernel(other, held, dense_out, blocks, sems):
@@ -187,25 +210,32 @@
     row = ((xh * N_FAR + z) * N_CORE + jnp.where(which == 1, core, 1 - core)) * N_EDP + e
     place = (jnp.arange(ROWS)[:, None] == row).astype(bf16)
 
-    acts = lax.dot_general(
-        dense_acts, place, (((1,), (0,)), ((), ())), preferred_element_type=bf16
-    )
+    def picked(columns):
+        return lax.optimization_barrier(
+            lax.dot_general(
+                dense_acts, columns, (((1,), (0,)), ((), ())), preferred_element_type=bf16
+            )
+        )
+
     scaled = (advantage[:, None] * dense_cot.astype(f32)).astype(bf16)
 
     def product(a):
         return lax.dot_general(a, scaled, (((0,), (0,)), ((), ())), preferred_element_type=f32)
 
     swap = [(0, 1), (1, 0)]
-    received = lax.ppermute(product(acts[:, :HALF]).astype(bf16), "core", swap)
-    own = product(acts[:, HALF:])
+    received = lax.ppermute(product(picked(place[:, :HALF])).astype(bf16), "core", swap)
+    own = product(picked(place[:, HALF:]))
     near = sds((N_NEAR, PACKED_ROWS, W), bf16)
     far = sds((N_FAR, PIECE_ROWS, LANES), bf16)
     rows_r = sds((EXPERTS, 1, FF), f32)
     rows_d = sds((1, COLUMNS), f32)
-    sent = call(pack_kernel, near)(own, received, routed_grads.reshape(EXPERTS * N_EDP, FF))
+    routed_sent = call(routed_pack_kernel, sds((N_NEAR, 16, W), bf16), 64 << 20)(
+        routed_grads.reshape(EXPERTS * N_EDP, FF)
+    )
+    sent = call(pack_kernel, near)(own, received, routed_sent)
     got = exchange(sent, NEAR)
-    far_sent, routed_master_new, routed_first_new, routed_second_new, weights = call(
-        middle_kernel, (far, rows_r, rows_r, rows_r, sds((16, W), bf16))
+    far_sent, weights, routed_total = call(
+        middle_kernel, (far, sds((16, W), bf16), sds((16, W), f32))
     )(got, routed_master, routed_first, routed_second)
     got = exchange(far_sent, FAR)
 
@@ -217,15 +247,18 @@
 
     dense_args = (got, dense_master, dense_first, dense_second)
     far_sent = call(ahead, far)(*dense_args)
-    dense_master_new, dense_first_new, dense_second_new = call(state, (rows_d, rows_d, rows_d))(
-        *dense_args
+    (
+        dense_master_new,
+        dense_first_new,
+        dense_second_new,
+        routed_master_new,
+        routed_first_new,
+        routed_second_new,
+    ) = call(state, (rows_d, rows_d, rows_d, rows_r, rows_r, rows_r))(
+        *dense_args, routed_total, routed_master, routed_first, routed_second
     )
     got = exchange(far_sent, FAR)
-    near_sent = call(spread_kernel, near)(got, weights)
-    near_sent, dense_master_new, dense_first_new, dense_second_new = lax.optimization_barrier(
-        (near_sent, dense_master_new, dense_first_new, dense_second_new)
-    )
-    own = exchange(near_sent, NEAR)
+    own = exchange(call(spread_kernel, near)(got, weights), NEAR)
     other = lax.ppermute(own, "core", swap)
     dense_shape = sds((ROWS // 16, N_CORE, N_EDP, COLUMNS), bf16)
     anywhere = pl.BlockSpec(memory_space=pl.ANY)
@@ -241,11 +274,19 @@
     )
     held, routed_weights = pl.pallas_call(
         own_place_kernel,
-        in_specs=[vmem],
-        out_specs=[anywhere, vmem],
         out_shape=(dense_shape, sds((EXPERTS * N_EDP, FF), bf16)),
-        **place_params,
-    )(own)
+        grid_spec=pltpu.PrefetchScalarGridSpec(
+            num_scalar_prefetch=1,
+            grid=(1,),
+            in_specs=[pl.BlockSpec((N_NEAR, PACKED_ROWS, W), lambda i, c: (0, 0, 0))],
+            out_specs=[
+                pl.BlockSpec((ROWS // 16, 1, N_EDP, COLUMNS), lambda i, c: (0, c[0], 0, 0)),
+                pl.BlockSpec((EXPERTS * N_EDP, FF), lambda i, c: (0, 0)),
+            ],
+        ),
+        compiler_params=place_params["compiler_params"],
+        cost_estimate=place_params["cost_estimate"],
+    )(core[None], own)
     dense_weights = pl.pallas_call(
         other_place_kernel,
         in_specs=[vmem, anywhere],

time: 104 us -> 101 us (0.971)
  blocking collectives: 59 us -> 73.2 us
  waiting for transfers between devices: 12.4 us -> 0.39 us
  starting transfers between devices: 20.4 us -> 17.1 us
  Pallas kernels: 5.63 us -> 4.06 us
    all_to_all x3 -> x4, blocking collectives: 59 us -> 73.2 us  [exchange(): return lax.all_to_all(x, axes, 0, 0, tiled=False)]
    all_to_all x1 -> x0, waiting for transfers between devices: 10.9 us -> none  [exchange(): return lax.all_to_all(x, axes, 0, 0, tiled=False)]
    all_to_all x1 -> x0, starting transfers between devices: 3.5 us -> none  [exchange(): return lax.all_to_all(x, axes, 0, 0, tiled=False)]
    pallas_call x5 -> x6, Pallas kernels: 3.84 us -> 2.9 us  [the longest x1 1.3 us: per_device(): pl.pallas_call(own_place_kernel, out_shape=(dense_shape, sds((EXPERTS * N...]
  transfers between devices with their start and end apart: 3 -> 2, of which waited for: 3 -> 2; matrix products, arithmetic and copies ran while one was open for 1% -> 1% of each run, Pallas kernels for 2% -> 2%
where the time goes in v4:
time: 101 us
  blocking collectives  73.2 us (72%)
  starting transfers between devices  17.1 us (17%)
  matrix products  4.32 us (4%)
  Pallas kernels  4.06 us (4%)
    all_to_all x4, blocking collectives, exchange(): return lax.all_to_all(x, axes, 0, 0, tiled=False)  73.2 us
    ppermute x1, starting transfers between devices, per_device(): lax.ppermute(product(picked(place[:, :HALF])).astype(bf16), 'core', swap)  8.79 us
    ppermute x1, starting transfers between devices, per_device(): other = lax.ppermute(own, 'core', swap)  8.29 us
    dot_general x2, matrix products, product(): lax.dot_general(a, scaled, (((0,), (0,)), ((), ())), preferred_element_ty...  3.44 us
  transfers between devices with their start and end apart: 2, of which 2 were waited for; matrix products, arithmetic and copies ran while one was open for 1% of the time, Pallas kernels for 2%

profile of v4, /device:TPU:1, one launch (start us, length us, event | category | flops | bytes accessed | tf_op | source)
XLA Modules:
  0.0 101.0 jit_solution(16939961019726338155)
XLA Ops:
  0.6 0.0 copy-start
  0.7 0.2 iota_compare_fusion
  0.8 0.9 copy-done
  1.7 0.4 fusion.1
  2.2 0.0 copy-start.1
  2.2 0.0 copy-start.8
  2.2 0.0 copy-start.9
  2.2 2.6 %convolution_convert_fusion = bf16[256,1536]{1,0:T(8,128)(2,1)S(1)} fusion(bf16[640,256]{0,1:T(8,128)(2,1)S(1)} %fusion.1, bf16[640,1536]{1,0:T(8,128)(2,1)} %param.11, f32[640]{0:T(1024)} %param.12), kind=kOutput, calls=%fused_computation.1 | convolution fusion | flops 506658816 | bytes 3082752 | tf_op jit(solution)/shard_map/dot_general | solution.py:223
  4.8 8.8 %collective-permute-start = (bf16[256,1536]{1,0:T(8,128)(2,1)S(1)}, bf16[256,1536]{1,0:T(8,128)(2,1)S(1)}, u32[]{:S(2)}, u32[]{:S(2)}) collective-permute-start(bf16[256,1536]{1,0:T(8,128)(2,1)S(1)} %convolution_convert_fusion), channel_id=1, source_target_pairs={{0,8},{8,0},{1,9},{9,1},{2,10},{10,2},{3,11},{11,3},{4,12},{12,4},... | collective-permute-start | bytes 2359304 | tf_op jit(solution)/shard_map/ppermute | solution.py:226
  13.6 0.4 fusion
  14.0 0.0 copy-done.1
  14.0 0.4 shard_map.161.routed
  14.5 0.0 copy-done.8
  14.5 0.0 copy-done.9
  14.5 0.9 fusion.2.own
  15.4 0.1 collective-permute-done.received
  15.5 0.1 shard_map.162
  15.6 0.0 copy-start.2
  15.6 0.0 copy-start.3
  15.7 0.0 copy-start.4
  15.7 0.0 copy-start.5
  15.7 0.0 copy-start.6
  15.7 0.0 copy-start.7
  15.7 18.6 %all_to_all.20.got = bf16[16,64,512]{2,1,0:T(8,128)(2,1)S(1)} all-to-all(bf16[16,64,512]{2,1,0:T(8,128)(2,1)S(1)} %shard_map.162), channel_id=1, replica_groups=mesh['xh'=2,'z'=16,'core'=2,'xl'=2,'y'=4] {'xh','xl','y'}, dimensions={0} | all-to-all | bytes 2097152 | tf_op jit(solution)/shard_map/all_to_all | solution.py:45
  34.3 0.0 copy-done.2
  34.3 0.0 copy-done.3
  34.3 0.0 copy-done.4
  34.3 0.2 shard_map.163
  34.6 25.0 %all_to_all.21.refs_0_ = bf16[16,16,128]{2,1,0:T(8,128)(2,1)S(1)} all-to-all(bf16[16,16,128]{2,1,0:T(8,128)(2,1)S(1)} %get-tuple-element.19), channel_id=1, replica_groups=mesh['xh'=2,'z'=16,'core'=2,'xl'=2,'y'=4] {'z'}, dimensions={0} | all-to-all | bytes 131072 | tf_op jit(solution)/shard_map/all_to_all | solution.py:45
  59.6 0.0 copy-done.5
  59.6 0.0 copy-done.6
  59.6 0.0 copy-done.7
  59.6 0.1 shard_map.165
  59.7 14.3 %all_to_all.22.got = bf16[16,16,128]{2,1,0:T(8,128)(2,1)S(1)} all-to-all(bf16[16,16,128]{2,1,0:T(8,128)(2,1)S(1)} %shard_map.165), channel_id=1, replica_groups=mesh['xh'=2,'z'=16,'core'=2,'xl'=2,'y'=4] {'z'}, dimensions={0} | all-to-all | bytes 131072 | tf_op jit(solution)/shard_map/all_to_all | solution.py:45
  74.0 0.1 shard_map.166
  74.1 15.2 %all_to_all.23.own = bf16[16,64,512]{2,1,0:T(8,128)(2,1)S(1)} all-to-all(bf16[16,64,512]{2,1,0:T(8,128)(2,1)S(1)} %shard_map.166), channel_id=1, replica_groups=mesh['xh'=2,'z'=16,'core'=2,'xl'=2,'y'=4] {'xh','xl','y'}, dimensions={0} | all-to-all | bytes 2097152 | tf_op jit(solution)/shard_map/all_to_all | solution.py:45
  89.3 8.3 %collective-permute-start.1 = (bf16[16,64,512]{2,1,0:T(8,128)(2,1)S(1)}, bf16[16,64,512]{2,1,0:T(8,128)(2,1)S(1)}, u32[]{:S(2)}, u32[]{:S(2)}) collective-permute-start(bf16[16,64,512]{2,1,0:T(8,128)(2,1)S(1)} %all_to_all.23.own), channel_id=1, source_target_pairs={{0,8},{8,0},{1,9},{9,1},{2,10},{10,2},{3,11},{11,3},{4,12},{12,4},... | collective-permute-start | bytes 3145736 | tf_op jit(solution)/shard_map/ppermute | solution.py:262
  97.6 0.7 shard_map.164
  98.3 1.3 %shard_map.167 = (bf16[32,2,8,1536]{3,2,1,0:T(8,128)(2,1)}, bf16[32,2048]{1,0:T(8,128)(2,1)}) custom-call(s32[1]{0:T(128)} %bitcast.3.core, bf16[16,64,512]{2,1,0:T(8,128)(2,1)S(1)} %all_to_all.23.own), custom_call_target="tpu_custom_call" | custom-call | flops 209715200 | bytes 2097152 | tf_op jit(solution)/shard_map/pallas_call | solution.py:275
  99.6 0.3 collective-permute-done.1.other
  99.9 1.1 %shard_map.168 = bf16[32,2,8,1536]{3,2,1,0:T(8,128)(2,1)} custom-call(bf16[16,64,512]{2,1,0:T(8,128)(2,1)S(1)} %collective-permute-done.1.other, bf16[32,2,8,1536]{3,2,1,0:T(8,128)(2,1)} %get-tuple-element.25.held), custom_call_target="tpu_custom_call", output_to_operand_aliasing={{}: (1, {})} | custom-call | flops 209715200 | bytes 2097152 | tf_op jit(solution)/shard_map/pallas_call | solution.py:290
  (1 shorter events, 0.0 us)
Async XLA Ops:
  0.6 1.1 %copy-start = (bf16[640,512]{1,0:T(8,128)(2,1)S(1)}, bf16[640,512]{1,0:T(8,128)(2,1)}, u32[]{:S(2)}) copy-start(bf16[640,512]{1,0:T(8,128)(2,1)} %param.10) | copy-start | bytes 1966084
  2.2 11.9 %copy-start.1 = (bf16[1,4,8,2048]{3,2,1,0:T(8,128)(2,1)S(1)}, bf16[1,4,8,2048]{3,2,1,0:T(8,128)(2,1)}, u32[]{:S(2)}) copy-start(bf16[1,4,8,2048]{3,2,1,0:T(8,128)(2,1)} %param.16) | copy-start | bytes 393220
  2.2 12.3 %copy-start.8 = (bf16[640,1536]{1,0:T(8,128)(2,1)S(1)}, bf16[640,1536]{1,0:T(8,128)(2,1)}, u32[]{:S(2)}) copy-start(bf16[640,1536]{1,0:T(8,128)(2,1)} %param.11) | copy-start | bytes 5898244
  2.2 12.3 %copy-start.9 = (f32[640]{0:T(1024)S(1)}, f32[640]{0:T(1024)}, u32[]{:S(2)}) copy-start(f32[640]{0:T(1024)} %param.12) | copy-start | bytes 7684
  4.8 10.7 %collective-permute-start = (bf16[256,1536]{1,0:T(8,128)(2,1)S(1)}, bf16[256,1536]{1,0:T(8,128)(2,1)S(1)}, u32[]{:S(2)}, u32[]{:S(2)}) collective-permute-start(bf16[256,1536]{1,0:T(8,128)(2,1)S(1)} %convolution_convert_fusion), channel_id=1, source_target_pairs={{0,8},{8,0},{1,9},{9,1},{2,10},{10,2},{3,11},{11,3},{4,12},{12,4},... | collective-permute-start | bytes 2359304 | tf_op jit(solution)/shard_map/ppermute | solution.py:226
  15.6 18.7 %copy-start.2 = (f32[4,1,2048]{2,1,0:T(1,128)S(1)}, f32[4,1,2048]{2,1,0:T(1,128)}, u32[]{:S(2)}) copy-start(f32[4,1,2048]{2,1,0:T(1,128)} %refs_5_.1) | copy-start | bytes 98308
  15.6 18.7 %copy-start.3 = (f32[4,1,2048]{2,1,0:T(1,128)S(1)}, f32[4,1,2048]{2,1,0:T(1,128)}, u32[]{:S(2)}) copy-start(f32[4,1,2048]{2,1,0:T(1,128)} %refs_6_.1) | copy-start | bytes 98308
  15.7 18.7 %copy-start.4 = (f32[4,1,2048]{2,1,0:T(1,128)S(1)}, f32[4,1,2048]{2,1,0:T(1,128)}, u32[]{:S(2)}) copy-start(f32[4,1,2048]{2,1,0:T(1,128)} %refs_7_.1) | copy-start | bytes 98308
  15.7 44.0 %copy-start.5 = (f32[1,1536]{1,0:T(1,128)S(1)}, f32[1,1536]{1,0:T(1,128)}, u32[]{:S(2)}) copy-start(f32[1,1536]{1,0:T(1,128)} %refs_1_.3) | copy-start | bytes 18436
  15.7 44.0 %copy-start.6 = (f32[1,1536]{1,0:T(1,128)S(1)}, f32[1,1536]{1,0:T(1,128)}, u32[]{:S(2)}) copy-start(f32[1,1536]{1,0:T(1,128)} %refs_2_.3) | copy-start | bytes 18436
  15.7 44.0 %copy-start.7 = (f32[1,1536]{1,0:T(1,128)S(1)}, f32[1,1536]{1,0:T(1,128)}, u32[]{:S(2)}) copy-start(f32[1,1536]{1,0:T(1,128)} %refs_3_.3) | copy-start | bytes 18436
  89.3 10.6 %collective-permute-start.1 = (bf16[16,64,512]{2,1,0:T(8,128)(2,1)S(1)}, bf16[16,64,512]{2,1,0:T(8,128)(2,1)S(1)}, u32[]{:S(2)}, u32[]{:S(2)}) collective-permute-start(bf16[16,64,512]{2,1,0:T(8,128)(2,1)S(1)} %all_to_all.23.own), channel_id=1, source_target_pairs={{0,8},{8,0},{1,9},{9,1},{2,10},{10,2},{3,11},{11,3},{4,12},{12,4},... | collective-permute-start | bytes 3145736 | tf_op jit(solution)/shard_map/ppermute | solution.py:262

commit v5 on v4

--- a/solution.py
+++ b/solution.py
@@ -17,7 +17,7 @@
 SIZES = (2, 16, 2, 2, 4)
 EP = ("xh", "z", "core")
 EDP = ("xl", "y")
-NEAR = ("xh", "xl", "y")
+NEAR = ("xl", "xh", "y")
 FAR = ("z",)
 N_NEAR, N_FAR, N_EDP, N_CORE, N_XH, N_DEV = 16, 16, 8, 2, 2, 512
 ROWS, COLUMNS, EXPERTS, FF = 512, 1536, 4, 2048
@@ -45,6 +45,16 @@
     return lax.all_to_all(x, axes, 0, 0, tiled=False)
 
 
+def chip(d):
+    return d // 4 % N_XH, d // N_EDP * 4 + d % 4
+
+
+def of_half(packed, x, i):
+    rows = slice(i * N_FAR, (i + 1) * N_FAR)
+    parts = [packed[at : at + 4, rows, :] for at in (x * 4, N_EDP + x * 4)]
+    return jnp.concatenate(parts, axis=0).reshape(N_EDP * N_FAR, W)
+
+
 def iota(shape, dim):
     return lax.broadcasted_iota(jnp.int32, shape, dim)
 
@@ -63,7 +73,8 @@
     xh = lax.axis_index("xh")
     shape = (N_NEAR * 16, EXPERTS * N_EDP)
     q, c = iota(shape, 0), iota(shape, 1)
-    same = (q // 128 == xh) & (q // 16 % N_EDP == c % N_EDP) & (q % EXPERTS == c // N_EDP)
+    half, e = chip(q // 16)
+    same = (half == xh) & (e == c % N_EDP) & (q % EXPERTS == c // N_EDP)
     total = jnp.zeros((N_NEAR * 16, W), f32)
     for b in range(N_ROUTED):
         pick = jnp.where(same & (q // EXPERTS % N_ROUTED == b), 1.0, 0.0).astype(bf16)
@@ -147,13 +158,11 @@
 
 
 def place_rows(packed, core, out, blocks, sems):
-    n = N_EDP * N_FAR
     place = place_matrix()
     copies = []
     for x in range(N_XH):
         for i in range(N_DENSE):
-            rows = packed[x * N_EDP : (x + 1) * N_EDP, i * N_FAR : (i + 1) * N_FAR, :]
-            block = jnp.dot(place, rows.reshape(n, W), preferred_element_type=f32)
+            block = jnp.dot(place, of_half(packed, x, i), preferred_element_type=f32)
             k = x * N_DENSE + i
             blocks[k] = block.reshape(N_FAR, N_EDP, W).astype(bf16)
             to = out.at[pl.ds(x * N_FAR, N_FAR), core, :, pl.ds(i * W, W)]
@@ -163,19 +172,18 @@
 
 
 def own_place_kernel(core, own, dense_out, routed_out):
-    n = N_EDP * N_FAR
     place = place_matrix()
     for x in range(N_XH):
         for i in range(N_DENSE):
-            rows = own[x * N_EDP : (x + 1) * N_EDP, i * N_FAR : (i + 1) * N_FAR, :]
-            block = jnp.dot(place, rows.reshape(n, W), preferred_element_type=f32)
+            block = jnp.dot(place, of_half(own, x, i), preferred_element_type=f32)
             dense_out[x * N_FAR : (x + 1) * N_FAR, 0, :, i * W : (i + 1) * W] = block.reshape(
                 N_FAR, N_EDP, W
             ).astype(bf16)
     xh = lax.axis_index("xh")
     shape = (EXPERTS * N_EDP, N_NEAR * 16)
     c, q = iota(shape, 0), iota(shape, 1)
-    same = (q // 128 == xh) & (q // 16 % N_EDP == c % N_EDP) & (q % EXPERTS == c // N_EDP)
+    half, e = chip(q // 16)
+    same = (half == xh) & (e == c % N_EDP) & (q % EXPERTS == c // N_EDP)
     packed = own[:, DENSE_ROWS:, :].reshape(N_NEAR * 16, W)
     for b in range(N_ROUTED):
         pick = jnp.where(same & (q // EXPERTS % N_ROUTED == b), 1.0, 0.0).astype(bf16)
@@ -206,7 +214,8 @@
     sds = jax.ShapeDtypeStruct
 
     packed = jnp.arange(ROWS)[None, :]
-    which, xh, e, z = packed // HALF, packed // 128 % N_XH, packed // N_FAR % N_EDP, packed % N_FAR
+    which, z = packed // HALF, packed % N_FAR
+    xh, e = chip(packed // N_FAR % N_NEAR)
     row = ((xh * N_FAR + z) * N_CORE + jnp.where(which == 1, core, 1 - core)) * N_EDP + e
     place = (jnp.arange(ROWS)[:, None] == row).astype(bf16)
 

time: 101 us -> 101 us (level)
  no operation moved by 1% of the time
where the time goes in v5:
time: 101 us; the launch traced here: 100 us
  blocking collectives  72.9 us (72%)
  starting transfers between devices  16.6 us (16%)
  matrix products  4.33 us (4%)
  Pallas kernels  4.06 us (4%)
    all_to_all x4, blocking collectives, exchange(): return lax.all_to_all(x, axes, 0, 0, tiled=False)  72.9 us
    ppermute x1, starting transfers between devices, per_device(): lax.ppermute(product(picked(place[:, :HALF])).astype(bf16), 'core', swap)  8.79 us
    ppermute x1, starting transfers between devices, per_device(): other = lax.ppermute(own, 'core', swap)  7.78 us
    dot_general x2, matrix products, product(): lax.dot_general(a, scaled, (((0,), (0,)), ((), ())), preferred_element_ty...  3.46 us
  transfers between devices with their start and end apart: 2, of which 2 were waited for; matrix products, arithmetic and copies ran while one was open for 1% of the time, Pallas kernels for 2%

profile of v5, /device:TPU:1, one launch (start us, length us, event | category | flops | bytes accessed | tf_op | source)
XLA Modules:
  0.0 100.2 jit_solution(2230531111764249670)
XLA Ops:
  0.6 0.0 copy-start
  0.7 0.2 iota_compare_fusion
  0.8 0.9 copy-done
  1.7 0.4 fusion.1
  2.2 0.0 copy-start.1
  2.2 0.0 copy-start.8
  2.2 0.0 copy-start.9
  2.2 2.6 %convolution_convert_fusion = bf16[256,1536]{1,0:T(8,128)(2,1)S(1)} fusion(bf16[640,256]{0,1:T(8,128)(2,1)S(1)} %fusion.1, bf16[640,1536]{1,0:T(8,128)(2,1)} %param.11, f32[640]{0:T(1024)} %param.12), kind=kOutput, calls=%fused_computation.1 | convolution fusion | flops 506658816 | bytes 3082752 | tf_op jit(solution)/shard_map/dot_general | solution.py:232
  4.8 8.8 %collective-permute-start = (bf16[256,1536]{1,0:T(8,128)(2,1)S(1)}, bf16[256,1536]{1,0:T(8,128)(2,1)S(1)}, u32[]{:S(2)}, u32[]{:S(2)}) collective-permute-start(bf16[256,1536]{1,0:T(8,128)(2,1)S(1)} %convolution_convert_fusion), channel_id=1, source_target_pairs={{0,8},{8,0},{1,9},{9,1},{2,10},{10,2},{3,11},{11,3},{4,12},{12,4},... | collective-permute-start | bytes 2359304 | tf_op jit(solution)/shard_map/ppermute | solution.py:235
  13.6 0.4 fusion
  14.0 0.0 copy-done.1
  14.0 0.4 shard_map.161.routed
  14.5 0.0 copy-done.8
  14.5 0.0 copy-done.9
  14.5 0.9 fusion.2.own
  15.4 0.1 collective-permute-done.received
  15.5 0.1 shard_map.162
  15.6 0.0 copy-start.2
  15.6 0.0 copy-start.3
  15.7 0.0 copy-start.4
  15.7 0.0 copy-start.5
  15.7 0.0 copy-start.6
  15.7 0.0 copy-start.7
  15.7 18.6 %all_to_all.20.got = bf16[16,64,512]{2,1,0:T(8,128)(2,1)S(1)} all-to-all(bf16[16,64,512]{2,1,0:T(8,128)(2,1)S(1)} %shard_map.162), channel_id=1, replica_groups=mesh['xh'=2,'z'=16,'core'=2,'xl'=2,'y'=4] {'xl','xh','y'}, dimensions={0} | all-to-all | bytes 2097152 | tf_op jit(solution)/shard_map/all_to_all | solution.py:45
  34.3 0.0 copy-done.2
  34.3 0.0 copy-done.3
  34.3 0.0 copy-done.4
  34.3 0.2 shard_map.163
  34.5 24.8 %all_to_all.21.refs_0_ = bf16[16,16,128]{2,1,0:T(8,128)(2,1)S(1)} all-to-all(bf16[16,16,128]{2,1,0:T(8,128)(2,1)S(1)} %get-tuple-element.19), channel_id=1, replica_groups=mesh['xh'=2,'z'=16,'core'=2,'xl'=2,'y'=4] {'z'}, dimensions={0} | all-to-all | bytes 131072 | tf_op jit(solution)/shard_map/all_to_all | solution.py:45
  59.3 0.0 copy-done.5
  59.3 0.0 copy-done.6
  59.3 0.0 copy-done.7
  59.3 0.1 shard_map.165
  59.4 14.4 %all_to_all.22.got = bf16[16,16,128]{2,1,0:T(8,128)(2,1)S(1)} all-to-all(bf16[16,16,128]{2,1,0:T(8,128)(2,1)S(1)} %shard_map.165), channel_id=1, replica_groups=mesh['xh'=2,'z'=16,'core'=2,'xl'=2,'y'=4] {'z'}, dimensions={0} | all-to-all | bytes 131072 | tf_op jit(solution)/shard_map/all_to_all | solution.py:45
  73.8 0.1 shard_map.166
  73.9 15.2 %all_to_all.23.own = bf16[16,64,512]{2,1,0:T(8,128)(2,1)S(1)} all-to-all(bf16[16,64,512]{2,1,0:T(8,128)(2,1)S(1)} %shard_map.166), channel_id=1, replica_groups=mesh['xh'=2,'z'=16,'core'=2,'xl'=2,'y'=4] {'xl','xh','y'}, dimensions={0} | all-to-all | bytes 2097152 | tf_op jit(solution)/shard_map/all_to_all | solution.py:45
  89.0 7.8 %collective-permute-start.1 = (bf16[16,64,512]{2,1,0:T(8,128)(2,1)S(1)}, bf16[16,64,512]{2,1,0:T(8,128)(2,1)S(1)}, u32[]{:S(2)}, u32[]{:S(2)}) collective-permute-start(bf16[16,64,512]{2,1,0:T(8,128)(2,1)S(1)} %all_to_all.23.own), channel_id=1, source_target_pairs={{0,8},{8,0},{1,9},{9,1},{2,10},{10,2},{3,11},{11,3},{4,12},{12,4},... | collective-permute-start | bytes 3145736 | tf_op jit(solution)/shard_map/ppermute | solution.py:271
  96.8 0.7 shard_map.164
  97.5 1.3 %shard_map.167 = (bf16[32,2,8,1536]{3,2,1,0:T(8,128)(2,1)}, bf16[32,2048]{1,0:T(8,128)(2,1)}) custom-call(s32[1]{0:T(128)} %bitcast.3.core, bf16[16,64,512]{2,1,0:T(8,128)(2,1)S(1)} %all_to_all.23.own), custom_call_target="tpu_custom_call" | custom-call | flops 209715200 | bytes 2097152 | tf_op jit(solution)/shard_map/pallas_call | solution.py:284
  98.8 0.3 collective-permute-done.1.other
  99.1 1.1 %shard_map.168 = bf16[32,2,8,1536]{3,2,1,0:T(8,128)(2,1)} custom-call(bf16[16,64,512]{2,1,0:T(8,128)(2,1)S(1)} %collective-permute-done.1.other, bf16[32,2,8,1536]{3,2,1,0:T(8,128)(2,1)} %get-tuple-element.25.held), custom_call_target="tpu_custom_call", output_to_operand_aliasing={{}: (1, {})} | custom-call | flops 209715200 | bytes 2097152 | tf_op jit(solution)/shard_map/pallas_call | solution.py:299
  (1 shorter events, 0.0 us)
Async XLA Ops:
  0.6 1.1 %copy-start = (bf16[640,512]{1,0:T(8,128)(2,1)S(1)}, bf16[640,512]{1,0:T(8,128)(2,1)}, u32[]{:S(2)}) copy-start(bf16[640,512]{1,0:T(8,128)(2,1)} %param.10) | copy-start | bytes 1966084
  2.2 11.9 %copy-start.1 = (bf16[1,4,8,2048]{3,2,1,0:T(8,128)(2,1)S(1)}, bf16[1,4,8,2048]{3,2,1,0:T(8,128)(2,1)}, u32[]{:S(2)}) copy-start(bf16[1,4,8,2048]{3,2,1,0:T(8,128)(2,1)} %param.16) | copy-start | bytes 393220
  2.2 12.3 %copy-start.8 = (bf16[640,1536]{1,0:T(8,128)(2,1)S(1)}, bf16[640,1536]{1,0:T(8,128)(2,1)}, u32[]{:S(2)}) copy-start(bf16[640,1536]{1,0:T(8,128)(2,1)} %param.11) | copy-start | bytes 5898244
  2.2 12.3 %copy-start.9 = (f32[640]{0:T(1024)S(1)}, f32[640]{0:T(1024)}, u32[]{:S(2)}) copy-start(f32[640]{0:T(1024)} %param.12) | copy-start | bytes 7684
  4.8 10.7 %collective-permute-start = (bf16[256,1536]{1,0:T(8,128)(2,1)S(1)}, bf16[256,1536]{1,0:T(8,128)(2,1)S(1)}, u32[]{:S(2)}, u32[]{:S(2)}) collective-permute-start(bf16[256,1536]{1,0:T(8,128)(2,1)S(1)} %convolution_convert_fusion), channel_id=1, source_target_pairs={{0,8},{8,0},{1,9},{9,1},{2,10},{10,2},{3,11},{11,3},{4,12},{12,4},... | collective-permute-start | bytes 2359304 | tf_op jit(solution)/shard_map/ppermute | solution.py:235
  15.6 18.6 %copy-start.2 = (f32[4,1,2048]{2,1,0:T(1,128)S(1)}, f32[4,1,2048]{2,1,0:T(1,128)}, u32[]{:S(2)}) copy-start(f32[4,1,2048]{2,1,0:T(1,128)} %refs_5_.1) | copy-start | bytes 98308
  15.6 18.6 %copy-start.3 = (f32[4,1,2048]{2,1,0:T(1,128)S(1)}, f32[4,1,2048]{2,1,0:T(1,128)}, u32[]{:S(2)}) copy-start(f32[4,1,2048]{2,1,0:T(1,128)} %refs_6_.1) | copy-start | bytes 98308
  15.7 18.6 %copy-start.4 = (f32[4,1,2048]{2,1,0:T(1,128)S(1)}, f32[4,1,2048]{2,1,0:T(1,128)}, u32[]{:S(2)}) copy-start(f32[4,1,2048]{2,1,0:T(1,128)} %refs_7_.1) | copy-start | bytes 98308
  15.7 43.7 %copy-start.5 = (f32[1,1536]{1,0:T(1,128)S(1)}, f32[1,1536]{1,0:T(1,128)}, u32[]{:S(2)}) copy-start(f32[1,1536]{1,0:T(1,128)} %refs_1_.3) | copy-start | bytes 18436
  15.7 43.7 %copy-start.6 = (f32[1,1536]{1,0:T(1,128)S(1)}, f32[1,1536]{1,0:T(1,128)}, u32[]{:S(2)}) copy-start(f32[1,1536]{1,0:T(1,128)} %refs_2_.3) | copy-start | bytes 18436
  15.7 43.7 %copy-start.7 = (f32[1,1536]{1,0:T(1,128)S(1)}, f32[1,1536]{1,0:T(1,128)}, u32[]{:S(2)}) copy-start(f32[1,1536]{1,0:T(1,128)} %refs_3_.3) | copy-start | bytes 18436
  89.0 10.1 %collective-permute-start.1 = (bf16[16,64,512]{2,1,0:T(8,128)(2,1)S(1)}, bf16[16,64,512]{2,1,0:T(8,128)(2,1)S(1)}, u32[]{:S(2)}, u32[]{:S(2)}) collective-permute-start(bf16[16,64,512]{2,1,0:T(8,128)(2,1)S(1)} %all_to_all.23.own), channel_id=1, source_target_pairs={{0,8},{8,0},{1,9},{9,1},{2,10},{10,2},{3,11},{11,3},{4,12},{12,4},... | collective-permute-start | bytes 3145736 | tf_op jit(solution)/shard_map/ppermute | solution.py:271

commit v6 on v5

--- a/solution.py
+++ b/solution.py
@@ -13,12 +13,12 @@
 decay_rate = 0.1
 epsilon = 1e-08
 
-AXES = ("xh", "z", "core", "xl", "y")
-SIZES = (2, 16, 2, 2, 4)
-EP = ("xh", "z", "core")
+AXES = ("xh", "zh", "zl", "core", "xl", "y")
+SIZES = (2, 4, 4, 2, 2, 4)
+EP = ("xh", "zh", "zl", "core")
 EDP = ("xl", "y")
 NEAR = ("xl", "xh", "y")
-FAR = ("z",)
+FAR = ("zl", "zh")
 N_NEAR, N_FAR, N_EDP, N_CORE, N_XH, N_DEV = 16, 16, 8, 2, 2, 512
 ROWS, COLUMNS, EXPERTS, FF = 512, 1536, 4, 2048
 HALF = ROWS // 2
@@ -47,6 +47,10 @@
 
 def chip(d):
     return d // 4 % N_XH, d // N_EDP * 4 + d % 4
+
+
+def level(p):
+    return p % 4 * 4 + p // 4
 
 
 def of_half(packed, x, i):
@@ -153,7 +157,7 @@
 def place_matrix():
     n = N_EDP * N_FAR
     p, q = iota((n, n), 0), iota((n, n), 1)
-    same = (p // N_EDP == q % N_FAR) & (p % N_EDP == q // N_FAR)
+    same = (p // N_EDP == level(q % N_FAR)) & (p % N_EDP == q // N_FAR)
     return jnp.where(same, 1.0, 0.0).astype(bf16)
 
 
@@ -214,7 +218,7 @@
     sds = jax.ShapeDtypeStruct
 
     packed = jnp.arange(ROWS)[None, :]
-    which, z = packed // HALF, packed % N_FAR
+    which, z = packed // HALF, level(packed % N_FAR)
     xh, e = chip(packed // N_FAR % N_NEAR)
     row = ((xh * N_FAR + z) * N_CORE + jnp.where(which == 1, core, 1 - core)) * N_EDP + e
     place = (jnp.arange(ROWS)[:, None] == row).astype(bf16)

time: 101 us -> 101 us (level)
  no operation moved by 1% of the time
where the time goes in v6:
time: 101 us; the launch traced here: 100 us
  blocking collectives  73.1 us (72%)
  starting transfers between devices  16.5 us (16%)
  matrix products  4.33 us (4%)
  Pallas kernels  4.05 us (4%)
    all_to_all x4, blocking collectives, exchange(): return lax.all_to_all(x, axes, 0, 0, tiled=False)  73.1 us
    ppermute x1, starting transfers between devices, per_device(): lax.ppermute(product(picked(place[:, :HALF])).astype(bf16), 'core', swap)  8.79 us
    ppermute x1, starting transfers between devices, per_device(): other = lax.ppermute(own, 'core', swap)  7.68 us
    dot_general x2, matrix products, product(): lax.dot_general(a, scaled, (((0,), (0,)), ((), ())), preferred_element_ty...  3.46 us
  transfers between devices with their start and end apart: 2, of which 2 were waited for; matrix products, arithmetic and copies ran while one was open for 1% of the time, Pallas kernels for 2%

profile of v6, /device:TPU:1, one launch (start us, length us, event | category | flops | bytes accessed | tf_op | source)
XLA Modules:
  0.0 100.3 jit_solution(15135143354033784077)
XLA Ops:
  0.6 0.0 copy-start
  0.7 0.2 iota_compare_fusion
  0.8 0.9 copy-done
  1.7 0.4 fusion.1
  2.2 0.0 copy-start.1
  2.2 0.0 copy-start.8
  2.2 0.0 copy-start.9
  2.2 2.6 %convolution_convert_fusion = bf16[256,1536]{1,0:T(8,128)(2,1)S(1)} fusion(bf16[640,256]{0,1:T(8,128)(2,1)S(1)} %fusion.1, bf16[640,1536]{1,0:T(8,128)(2,1)} %param.11, f32[640]{0:T(1024)} %param.12), kind=kOutput, calls=%fused_computation.1 | convolution fusion | flops 506658816 | bytes 3082752 | tf_op jit(solution)/shard_map/dot_general | solution.py:236
  4.8 8.8 %collective-permute-start = (bf16[256,1536]{1,0:T(8,128)(2,1)S(1)}, bf16[256,1536]{1,0:T(8,128)(2,1)S(1)}, u32[]{:S(2)}, u32[]{:S(2)}) collective-permute-start(bf16[256,1536]{1,0:T(8,128)(2,1)S(1)} %convolution_convert_fusion), channel_id=1, source_target_pairs={{0,8},{8,0},{1,9},{9,1},{2,10},{10,2},{3,11},{11,3},{4,12},{12,4},... | collective-permute-start | bytes 2359304 | tf_op jit(solution)/shard_map/ppermute | solution.py:239
  13.6 0.4 fusion
  14.0 0.0 copy-done.1
  14.0 0.4 shard_map.161.routed
  14.5 0.0 copy-done.8
  14.5 0.0 copy-done.9
  14.5 0.9 fusion.2.own
  15.4 0.1 collective-permute-done.received
  15.5 0.1 shard_map.162
  15.6 0.0 copy-start.2
  15.6 0.0 copy-start.3
  15.7 0.0 copy-start.4
  15.7 0.0 copy-start.5
  15.7 0.0 copy-start.6
  15.7 0.0 copy-start.7
  15.7 18.6 %all_to_all.20.got = bf16[16,64,512]{2,1,0:T(8,128)(2,1)S(1)} all-to-all(bf16[16,64,512]{2,1,0:T(8,128)(2,1)S(1)} %shard_map.162), channel_id=1, replica_groups=mesh['xh'=2,'zh'=4,'zl'=4,'core'=2,'xl'=2,'y'=4] {'xl','xh','y'}, dimensions={0} | all-to-all | bytes 2097152 | tf_op jit(solution)/shard_map/all_to_all | solution.py:45
  34.3 0.0 copy-done.2
  34.3 0.0 copy-done.3
  34.3 0.0 copy-done.4
  34.3 0.2 shard_map.163
  34.5 24.9 %all_to_all.21.refs_0_ = bf16[16,16,128]{2,1,0:T(8,128)(2,1)S(1)} all-to-all(bf16[16,16,128]{2,1,0:T(8,128)(2,1)S(1)} %get-tuple-element.19), channel_id=1, replica_groups=mesh['xh'=2,'zh'=4,'zl'=4,'core'=2,'xl'=2,'y'=4] {'zl','zh'}, dimensions={0} | all-to-all | bytes 131072 | tf_op jit(solution)/shard_map/all_to_all | solution.py:45
  59.4 0.0 copy-done.5
  59.4 0.0 copy-done.6
  59.4 0.0 copy-done.7
  59.4 0.1 shard_map.165
  59.5 14.4 %all_to_all.22.got = bf16[16,16,128]{2,1,0:T(8,128)(2,1)S(1)} all-to-all(bf16[16,16,128]{2,1,0:T(8,128)(2,1)S(1)} %shard_map.165), channel_id=1, replica_groups=mesh['xh'=2,'zh'=4,'zl'=4,'core'=2,'xl'=2,'y'=4] {'zl','zh'}, dimensions={0} | all-to-all | bytes 131072 | tf_op jit(solution)/shard_map/all_to_all | solution.py:45
  73.9 0.1 shard_map.166
  74.0 15.2 %all_to_all.23.own = bf16[16,64,512]{2,1,0:T(8,128)(2,1)S(1)} all-to-all(bf16[16,64,512]{2,1,0:T(8,128)(2,1)S(1)} %shard_map.166), channel_id=1, replica_groups=mesh['xh'=2,'zh'=4,'zl'=4,'core'=2,'xl'=2,'y'=4] {'xl','xh','y'}, dimensions={0} | all-to-all | bytes 2097152 | tf_op jit(solution)/shard_map/all_to_all | solution.py:45
  89.2 7.7 %collective-permute-start.1 = (bf16[16,64,512]{2,1,0:T(8,128)(2,1)S(1)}, bf16[16,64,512]{2,1,0:T(8,128)(2,1)S(1)}, u32[]{:S(2)}, u32[]{:S(2)}) collective-permute-start(bf16[16,64,512]{2,1,0:T(8,128)(2,1)S(1)} %all_to_all.23.own), channel_id=1, source_target_pairs={{0,8},{8,0},{1,9},{9,1},{2,10},{10,2},{3,11},{11,3},{4,12},{12,4},... | collective-permute-start | bytes 3145736 | tf_op jit(solution)/shard_map/ppermute | solution.py:275
  96.9 0.7 shard_map.164
  97.6 1.3 %shard_map.167 = (bf16[32,2,8,1536]{3,2,1,0:T(8,128)(2,1)}, bf16[32,2048]{1,0:T(8,128)(2,1)}) custom-call(s32[1]{0:T(128)} %bitcast.3.core, bf16[16,64,512]{2,1,0:T(8,128)(2,1)S(1)} %all_to_all.23.own), custom_call_target="tpu_custom_call" | custom-call | flops 209715200 | bytes 2097152 | tf_op jit(solution)/shard_map/pallas_call | solution.py:288
  98.9 0.3 collective-permute-done.1.other
  99.2 1.1 %shard_map.168 = bf16[32,2,8,1536]{3,2,1,0:T(8,128)(2,1)} custom-call(bf16[16,64,512]{2,1,0:T(8,128)(2,1)S(1)} %collective-permute-done.1.other, bf16[32,2,8,1536]{3,2,1,0:T(8,128)(2,1)} %get-tuple-element.25.held), custom_call_target="tpu_custom_call", output_to_operand_aliasing={{}: (1, {})} | custom-call | flops 209715200 | bytes 2097152 | tf_op jit(solution)/shard_map/pallas_call | solution.py:303
  (1 shorter events, 0.0 us)
Async XLA Ops:
  0.6 1.1 %copy-start = (bf16[640,512]{1,0:T(8,128)(2,1)S(1)}, bf16[640,512]{1,0:T(8,128)(2,1)}, u32[]{:S(2)}) copy-start(bf16[640,512]{1,0:T(8,128)(2,1)} %param.10) | copy-start | bytes 1966084
  2.2 11.9 %copy-start.1 = (bf16[1,4,8,2048]{3,2,1,0:T(8,128)(2,1)S(1)}, bf16[1,4,8,2048]{3,2,1,0:T(8,128)(2,1)}, u32[]{:S(2)}) copy-start(bf16[1,4,8,2048]{3,2,1,0:T(8,128)(2,1)} %param.16) | copy-start | bytes 393220
  2.2 12.3 %copy-start.8 = (bf16[640,1536]{1,0:T(8,128)(2,1)S(1)}, bf16[640,1536]{1,0:T(8,128)(2,1)}, u32[]{:S(2)}) copy-start(bf16[640,1536]{1,0:T(8,128)(2,1)} %param.11) | copy-start | bytes 5898244
  2.2 12.3 %copy-start.9 = (f32[640]{0:T(1024)S(1)}, f32[640]{0:T(1024)}, u32[]{:S(2)}) copy-start(f32[640]{0:T(1024)} %param.12) | copy-start | bytes 7684
  4.8 10.7 %collective-permute-start = (bf16[256,1536]{1,0:T(8,128)(2,1)S(1)}, bf16[256,1536]{1,0:T(8,128)(2,1)S(1)}, u32[]{:S(2)}, u32[]{:S(2)}) collective-permute-start(bf16[256,1536]{1,0:T(8,128)(2,1)S(1)} %convolution_convert_fusion), channel_id=1, source_target_pairs={{0,8},{8,0},{1,9},{9,1},{2,10},{10,2},{3,11},{11,3},{4,12},{12,4},... | collective-permute-start | bytes 2359304 | tf_op jit(solution)/shard_map/ppermute | solution.py:239
  15.6 18.6 %copy-start.2 = (f32[4,1,2048]{2,1,0:T(1,128)S(1)}, f32[4,1,2048]{2,1,0:T(1,128)}, u32[]{:S(2)}) copy-start(f32[4,1,2048]{2,1,0:T(1,128)} %refs_5_.1) | copy-start | bytes 98308
  15.6 18.6 %copy-start.3 = (f32[4,1,2048]{2,1,0:T(1,128)S(1)}, f32[4,1,2048]{2,1,0:T(1,128)}, u32[]{:S(2)}) copy-start(f32[4,1,2048]{2,1,0:T(1,128)} %refs_6_.1) | copy-start | bytes 98308
  15.7 18.6 %copy-start.4 = (f32[4,1,2048]{2,1,0:T(1,128)S(1)}, f32[4,1,2048]{2,1,0:T(1,128)}, u32[]{:S(2)}) copy-start(f32[4,1,2048]{2,1,0:T(1,128)} %refs_7_.1) | copy-start | bytes 98308
  15.7 43.8 %copy-start.5 = (f32[1,1536]{1,0:T(1,128)S(1)}, f32[1,1536]{1,0:T(1,128)}, u32[]{:S(2)}) copy-start(f32[1,1536]{1,0:T(1,128)} %refs_1_.3) | copy-start | bytes 18436
  15.7 43.7 %copy-start.6 = (f32[1,1536]{1,0:T(1,128)S(1)}, f32[1,1536]{1,0:T(1,128)}, u32[]{:S(2)}) copy-start(f32[1,1536]{1,0:T(1,128)} %refs_2_.3) | copy-start | bytes 18436
  15.7 43.7 %copy-start.7 = (f32[1,1536]{1,0:T(1,128)S(1)}, f32[1,1536]{1,0:T(1,128)}, u32[]{:S(2)}) copy-start(f32[1,1536]{1,0:T(1,128)} %refs_3_.3) | copy-start | bytes 18436
  89.2 10.0 %collective-permute-start.1 = (bf16[16,64,512]{2,1,0:T(8,128)(2,1)S(1)}, bf16[16,64,512]{2,1,0:T(8,128)(2,1)S(1)}, u32[]{:S(2)}, u32[]{:S(2)}) collective-permute-start(bf16[16,64,512]{2,1,0:T(8,128)(2,1)S(1)} %all_to_all.23.own), channel_id=1, source_target_pairs={{0,8},{8,0},{1,9},{9,1},{2,10},{10,2},{3,11},{11,3},{4,12},{12,4},... | collective-permute-start | bytes 3145736 | tf_op jit(solution)/shard_map/ppermute | solution.py:275
